TPU v7x, 32 devices: a whole 2x2x4 slice. The times are simulated.
32 devices in a mesh: dp: 8 (over z, x), tensor: 4 (over y, core).
Axes of the slice: x: 2, y: 2, z: 4, core: 2. Of those that a mesh axis runs over, the one named last changes fastest.
Arguments:
- tokens: bfloat16 [8192, 1024], P('dp'), may hold values from -6 to 6
- positions: int32 [8192], P('dp'), may hold values from -1 to 1023, as said below
- attn_gain: bfloat16 [1024], P('dp'), may hold values from 0.5 to 1.5
- query_gain: bfloat16 [64], replicated, may hold values from 0.25 to 1.75
- key_gain: bfloat16 [64], replicated, may hold values from 0.25 to 1.75
- w_query: bfloat16 [1024, 1024], P('dp', 'tensor'), may hold values from -0.1875 to 0.1875
- w_key: bfloat16 [1024, 512], P('dp', 'tensor'), may hold values from -0.1875 to 0.1875
- w_value: bfloat16 [1024, 512], P('dp', 'tensor'), may hold values from -0.1875 to 0.1875
- w_out: bfloat16 [1024, 1024], P('tensor', 'dp'), may hold values from -2 to 2
- ffn_gain: bfloat16 [1024], P('dp'), may hold values from 0.5 to 1.5
- w_gate: bfloat16 [1024, 4608], P('dp', 'tensor'), may hold values from -0.1875 to 0.1875
- w_up: bfloat16 [1024, 4608], P('dp', 'tensor'), may hold values from -0.1875 to 0.1875
- w_down: bfloat16 [4608, 1024], P('tensor', 'dp'), may hold values from -0.09375 to 0.09375
- cotangent: bfloat16 [8192, 1024], P('dp'), may hold values from -6 to 6
Outputs:
- block_output: bfloat16 [8192, 1024], P(('dp', 'tensor'))
- input_grad: bfloat16 [8192, 1024], P(('dp', 'tensor'))
- grad_attn_gain: float32 [1024], P('dp')
- grad_query_gain: float32 [64], replicated
- grad_key_gain: float32 [64], replicated
- grad_w_query: float32 [1024, 1024], P('dp', 'tensor')
- grad_w_key: float32 [1024, 512], P('dp', 'tensor')
- grad_w_value: float32 [1024, 512], P('dp', 'tensor')
- grad_w_out: float32 [1024, 1024], P('tensor', 'dp')
- grad_ffn_gain: float32 [1024], P('dp')
- grad_w_gate: float32 [1024, 4608], P('dp', 'tensor')
- grad_w_up: float32 [1024, 4608], P('dp', 'tensor')
- grad_w_down: float32 [4608, 1024], P('tensor', 'dp')
Inputs may be any that keep to these rules, and one draw needn't show every extreme that they name: Each group of 1024 slots of one index of dp holds whole sequences packed from its first slot: positions count 0, 1, 2, ... within a sequence, and slots after the last sequence hold -1. Every group fills at least half of its slots, and one group holds a single sequence of all 1024 slots.
All inputs are finite; a program needn't handle non-finite values.
Results may differ from a plain program's by a relative error of at most 0.018.
Values may be sent and summed in bfloat16 or wider, within the bound.
No kernel may reach another device: no remote copies, remote signals or barrier semaphores. Data moves between devices by JAX's collectives and lax.ppermute only.
A program may use at most 128 MiB of HBM per device.

v0:
```python
import functools

import jax
import jax.numpy as jnp
import numpy as np
from jax import lax
from jax.experimental import pallas as pl
from jax.experimental.pallas import tpu as pltpu
from jax.sharding import PartitionSpec as P

HD = 64
LANES = 128
epsilon = 1e-05
rope_base = 1000000.0
score_scale = HD ** (-0.5)
bf16 = jnp.bfloat16
f32 = jnp.float32
whole_vmem = pl.BlockSpec(memory_space=pltpu.VMEM)
scalars = pl.BlockSpec(memory_space=pltpu.SMEM)


def product(left, right):
    return jnp.dot(left, right, preferred_element_type=f32)


def contract_rows(left, right):
    return lax.dot_general(left, right, (((0,), (0,)), ((), ())), preferred_element_type=f32)


def contract_cols(left, right):
    return lax.dot_general(left, right, (((1,), (1,)), ((), ())), preferred_element_type=f32)


def ring_order(count):
    return list(range(0, count, 2)) + list(range(count - 1, 0, -2))


def ring_pairs(count):
    order = ring_order(count)
    ahead = [(order[i], order[(i + 1) % count]) for i in range(count)]
    return ahead, [(b, a) for a, b in ahead]


def tied(first, others):
    flat = lax.optimization_barrier((*first, *others))
    return flat[: len(first)], flat[len(first) :]


def after(values, needed):
    return tied(values, needed)[0]


class RingGather:
    def __init__(self, block, count):
        self.count, self.step = count, 0
        self.blocks = [block] + [None] * (count - 1)
        self.moving = (block, block)

    def send(self):
        ahead, back = ring_pairs(self.count)
        up, down = self.moving
        self.step += 1
        if self.step == self.count // 2:
            up, down = up[:HD], down[HD:]
        self.moving = (lax.ppermute(up, "dp", ahead), lax.ppermute(down, "dp", back))
        self.keep()

    def keep(self):
        half = self.count // 2
        if self.step < half:
            self.blocks[self.count - self.step], self.blocks[self.step] = self.moving
        else:
            self.blocks[half] = self.moving

    def tie(self, *others):
        self.moving, others = tied(self.moving, others)
        self.keep()
        return others

    def pieces(self):
        half = self.count // 2
        return [*self.blocks[:half], *self.blocks[half], *self.blocks[half + 1 :]]


class RingScatter:
    def __init__(self, blocks, top, bottom, count):
        self.blocks, self.count, self.step = blocks, count, count // 2
        self.moving = (top, bottom)

    def send(self):
        ahead, back = ring_pairs(self.count)
        self.moving = (lax.ppermute(self.moving[0], "dp", ahead), lax.ppermute(self.moving[1], "dp", back))
        self.step -= 1

    def add(self):
        up, down = self.moving
        mine_up, mine_down = self.blocks(self.step), self.blocks(self.count - self.step)
        if self.step == self.count // 2 - 1:
            up = jnp.concatenate([add(mine_up[:HD], up), mine_up[HD:]], axis=0)
            down = jnp.concatenate([mine_down[:HD], add(mine_down[HD:], down)], axis=0)
        else:
            up, down = add(mine_up, up), add(mine_down, down)
        self.moving = (up, down)

    def tie(self, *others):
        self.moving, others = tied(self.moving, others)
        return others


def pieces_of(full):
    blocks = [full[k * LANES : (k + 1) * LANES] for k in range(full.shape[0] // LANES)]
    half = len(blocks) // 2
    return blocks[:half] + [blocks[half][:HD], blocks[half][HD:]] + blocks[half + 1 :]


def add(left, right):
    return (left.astype(f32) + right.astype(f32)).astype(bf16)


def swap(values, axis, bit):
    count = lax.axis_size(axis)
    return lax.ppermute(values, axis, [(i, i ^ bit) for i in range(count)])


def tensor_scatter(send, keep):
    rows = send.shape[0] // 2
    other = swap(send, "tensor", 1)
    far = swap(add(keep[rows:], other[rows:]), "tensor", 2)
    return other, far


def tensor_gather(mine):
    near = swap(mine, "tensor", 1)
    far = swap(mine, "tensor", 2)
    return near, swap(far, "tensor", 1), mine, far


def sum_all(values):
    for axis in ("tensor", "dp"):
        bit = 1
        while bit < lax.axis_size(axis):
            values = values + swap(values, axis, bit)
            bit *= 2
    return values


def column(place, k, count):
    if not count:
        return k * LANES
    spot = place[1] + k
    spot = jnp.where(spot >= count, spot - count, spot)
    return pl.multiple_of(jnp.where(spot < count // 2, 2 * spot, 2 * count - 1 - 2 * spot) * LANES, LANES)


def lane_ids(rows):
    return lax.broadcasted_iota(jnp.int32, (rows, LANES), 1)


def head_sums(values):
    row = lax.broadcasted_iota(jnp.int32, (LANES, LANES), 0) < HD
    col = lax.broadcasted_iota(jnp.int32, (LANES, LANES), 1) < HD
    ones = jnp.where(row == col, 1.0, 0.0).astype(bf16)
    high = values.astype(bf16)
    rest = (values - high.astype(f32)).astype(bf16)
    return product(high, ones) + product(rest, ones)


def turn(values, sign):
    first = (lane_ids(values.shape[0]) % HD) < HD // 2
    ahead = pltpu.roll(values, LANES - HD // 2, 1)
    behind = pltpu.roll(values, HD // 2, 1)
    return jnp.where(first, -sign * ahead, sign * behind)


def spread_heads(values, fill):
    low = lane_ids(values.shape[0]) < HD
    moved = pltpu.roll(values, HD, 1)
    return (
        jnp.where(low, values, fill),
        jnp.where(low, fill, moved),
        jnp.where(low, moved, fill),
        jnp.where(low, fill, values),
    )


def assemble(pieces, out):
    row = 0
    for k, piece in enumerate(pieces):
        count = HD if k in (4, 5) else LANES
        out[row : row + count, :] = piece[:count, :]
        row += count


def row_norm(values):
    inverse = lax.rsqrt(jnp.mean(values * values, axis=-1, keepdims=True) + epsilon)
    return values * inverse, inverse


def project_kernel(
    place, tokens, cos_part, sin_part, gain_q, gain_k, p0, p1, p2, p3, p4, p5, p6, p7, p8,
    weights_out, gains, normed_low, qkv, q_out, k_out, v_out, cosine, sine,
):
    blocks, size = 4, qkv.shape[0] // 4
    pieces = (p0, p1, p2, p3, p4, p5, p6, p7, p8)
    assemble(pieces, weights_out)
    column = 0
    for k, piece in enumerate(pieces):
        if k == 4:
            continue
        at = HD if k == 5 else LANES
        row = piece[at : at + 16, :].astype(f32)
        gains[0:1, column : column + LANES] = row[0:1, :LANES]
        gains[1:2, column : column + LANES] = row[0:1, LANES : 2 * LANES]
        column += LANES

    def project(a, carry):
        here = pl.ds(pl.multiple_of(a * size, size), size)
        normed, _ = row_norm(tokens[here, :].astype(f32))
        h = (normed * gains[0:1, :]).astype(bf16)
        normed_low[here, :] = h
        qkv[here, :] = product(h, weights_out[:, : 4 * LANES])
        return carry

    lax.fori_loop(0, blocks, project, 0)

    def prepare(a, carry):
        here = pl.ds(pl.multiple_of(a * size, size), size)
        there = pl.ds(pl.multiple_of((a ^ place[0]) * size, size), size)
        cos_here = jnp.concatenate([cos_part[here, :]] * 4, axis=1)
        sin_here = jnp.concatenate([sin_part[here, :]] * 4, axis=1)
        cosine[here, :], sine[here, :] = cos_here, sin_here

        def turned(x, gain):
            inverse = lax.rsqrt(head_sums(x * x) * (1.0 / HD) + epsilon)
            y = x * inverse * gain
            return y * cos_here + turn(y, 1.0) * sin_here

        for g in range(2):
            q = turned(qkv[there, g * LANES : (g + 1) * LANES], gain_q[...])
            q_out[here, g * LANES : (g + 1) * LANES] = (q.astype(bf16).astype(f32) * score_scale).astype(bf16)
        k = turned(qkv[there, 2 * LANES : 3 * LANES], gain_k[...]).astype(bf16)
        v = qkv[there, 3 * LANES : 4 * LANES].astype(bf16)
        k_out[here, :] = k
        v_out[here, :] = v
        return carry

    lax.fori_loop(0, blocks, prepare, 0)


def attention_kernel(
    place, places, weights, q_in, k_in, v_in, attended, inverse_total, send, keep, keys, values, total,
):
    blocks, size = 4, q_in.shape[0] // 4
    low = lane_ids(size) < HD

    def prepare(a, carry):
        here = pl.ds(pl.multiple_of(a * size, size), size)
        k, v = k_in[here, :].astype(f32), v_in[here, :].astype(f32)
        for h, (one, two) in enumerate(zip(spread_heads(k, 0.0), spread_heads(v, 1.0))):
            keys[h, here, :] = one.astype(bf16)
            values[h, here, :] = two.astype(bf16)
        return carry

    lax.fori_loop(0, blocks, prepare, 0)
    offset = lax.broadcasted_iota(jnp.int32, (size, size), 0) - lax.broadcasted_iota(jnp.int32, (size, size), 1)

    def query_block(i, carry):
        here = pl.ds(pl.multiple_of(i * size, size), size)
        there = pl.ds(pl.multiple_of((i ^ place[0]) * size, size), size)
        total[...] = jnp.zeros_like(total)
        reach_here = jnp.concatenate([jnp.maximum(places[here, :], 0)] * (size // LANES), axis=1)

        def key_block(j, inner):
            at = pl.ds(pl.multiple_of(j * size, size), size)
            distance = offset + (i - j) * size
            allowed = (distance >= 0) & (distance <= reach_here)
            for h in range(4):
                q = q_in[here, (h // 2) * LANES : (h // 2 + 1) * LANES]
                weights = jnp.where(allowed, jnp.exp(contract_cols(q, keys[h, at, :])), 0.0)
                total[h] += product(weights.astype(bf16), values[h, at, :])
            return inner

        lax.fori_loop(0, i + 1, key_block, 0)
        for g in range(2):
            first, second = total[2 * g], total[2 * g + 1]
            inverse = 1.0 / pltpu.roll(jnp.where(low, second, first), HD, 1)
            cols = slice(g * LANES, (g + 1) * LANES)
            attended[there, cols] = (jnp.where(low, first, second) * inverse).astype(bf16)
            inverse_total[here, cols] = inverse
        return carry

    lax.fori_loop(0, blocks, query_block, 0)
    for j, (out, half) in enumerate([(keep, 0), (send, 0), (keep, 1), (send, 1)]):
        rows = slice(j * size, (j + 1) * size)
        out[half * size : (half + 1) * size, :] = contract_cols(attended[rows, :], weights[:, 4 * LANES :]).astype(bf16)


def backward_kernel(
    place, places, weights, q_in, k_in, v_in, attended, inverse_total, near, near_far, mine, far,
    dq_out, dk_out, dv_out, grad_in, keys, values, keys_t, grad_scaled, grad_aug, dq_t, dk_sum, dv_sum,
):
    blocks, size = 4, q_in.shape[0] // 4
    lane = lane_ids(size)
    low = lane < HD
    for j, rows in enumerate((mine, near, far, near_far)):
        grad_in[j * size : (j + 1) * size, :] = product(rows[...], weights[:, 4 * LANES :]).astype(bf16)

    def prepare(a, carry):
        here = pl.ds(pl.multiple_of(a * size, size), size)
        there = pl.ds(pl.multiple_of((a ^ place[0]) * size, size), size)
        k = spread_heads(k_in[here, :].astype(f32), 0.0)
        v = spread_heads(v_in[here, :].astype(f32), 1.0)
        for h in range(4):
            keys[h, here, :] = k[h].astype(bf16)
            keys_t[h, a] = k[h].T.astype(bf16)
            values[h, here, :] = v[h].astype(bf16)
        for g in range(2):
            cols = slice(g * LANES, (g + 1) * LANES)
            upstream = grad_in[there, cols].astype(f32)
            inverse = inverse_total[here, cols]
            delta = head_sums(upstream * attended[there, cols].astype(f32)) * inverse
            scaled = upstream * inverse
            grad_scaled[here, cols] = scaled.astype(bf16)
            moved = -pltpu.roll(delta, HD, 1)
            high = moved.astype(bf16).astype(f32)
            spare = jnp.where(lane % HD == 0, high, jnp.where(lane % HD == 1, moved - high, 0.0))
            grad_aug[2 * g, here, :] = jnp.where(low, scaled, spare).astype(bf16)
            grad_aug[2 * g + 1, here, :] = jnp.where(low, spare, scaled).astype(bf16)
            dq_t[g, a] = jnp.zeros((LANES, size), f32)
        return carry

    lax.fori_loop(0, blocks, prepare, 0)
    offset = lax.broadcasted_iota(jnp.int32, (size, size), 1) - lax.broadcasted_iota(jnp.int32, (size, size), 0)

    def key_block(j, carry):
        at = pl.ds(pl.multiple_of(j * size, size), size)
        dk_sum[...] = jnp.zeros_like(dk_sum)
        dv_sum[...] = jnp.zeros_like(dv_sum)

        def query_block(i, inner):
            here = pl.ds(pl.multiple_of(i * size, size), size)
            distance = offset + (i - j) * size
            allowed = (distance >= 0) & (distance <= jnp.maximum(places[i], 0))
            for g in range(2):
                cols = slice(g * LANES, (g + 1) * LANES)
                q = q_in[here, cols]
                upstream = grad_scaled[here, cols]
                dk_parts, dv_parts, dq_parts = [], [], []
                for h in (2 * g, 2 * g + 1):
                    weights_t = jnp.where(allowed, jnp.exp(contract_cols(keys[h, at, :], q)), 0.0)
                    share_grad = contract_cols(values[h, at, :], grad_aug[h, here, :])
                    score_grad = (weights_t * share_grad).astype(bf16)
                    dv_parts.append(product(weights_t.astype(bf16), upstream))
                    dk_parts.append(product(score_grad, q))
                    dq_parts.append(product(keys_t[h, j], score_grad))
                dq_t[g, i] += dq_parts[0] + dq_parts[1]
                dk_sum[g] += jnp.where(low, dk_parts[0], dk_parts[1])
                dv_sum[g] += jnp.where(low, dv_parts[0], dv_parts[1])
            return inner

        lax.fori_loop(j, blocks, query_block, 0)

        def folded(sums):
            both = [sums[g] + pltpu.roll(sums[g], HD, 1) for g in range(2)]
            return jnp.where(low, both[0], both[1])

        dk_out[at, :] = folded(dk_sum)
        dv_out[at, :] = folded(dv_sum).astype(bf16)
        return carry

    lax.fori_loop(0, blocks, key_block, 0)

    def finish(a, carry):
        here = pl.ds(pl.multiple_of(a * size, size), size)
        for g in range(2):
            dq_out[here, g * LANES : (g + 1) * LANES] = dq_t[g, a].T * score_scale
        return carry

    lax.fori_loop(0, blocks, finish, 0)


def backward_end_kernel(
    ring, place, tokens, weights, normed_low, qkv, cosine, sine, gain_q, gain_k, attended,
    near, near_far, mine, far, ffn_gain, dq, dk, dv,
    grad_weights, top, bottom, send, keep, grad_attn, grad_gain, grad_qkv,
):
    blocks, size = 4, qkv.shape[0] // 4
    grad_gain[...] = jnp.zeros_like(grad_gain)

    def finish(a, carry):
        here = pl.ds(pl.multiple_of(a * size, size), size)
        there = pl.ds(pl.multiple_of((a ^ place[0]) * size, size), size)
        cos_here, sin_here = cosine[here, :], sine[here, :]
        for part in range(3):
            cols = slice(part * LANES, (part + 1) * LANES)
            gain = gain_q[...] if part < 2 else gain_k[...]
            upstream = dq[here, cols] if part < 2 else dk[here, :]
            upstream = upstream * cos_here - turn(upstream * sin_here, 1.0)
            x = qkv[there, cols]
            inverse = lax.rsqrt(head_sums(x * x) * (1.0 / HD) + epsilon)
            normed = x * inverse
            scaled = upstream * gain
            inner_sum = head_sums(scaled * normed) * (1.0 / HD)
            grad_qkv[there, cols] = (inverse * (scaled - normed * inner_sum)).astype(bf16)
            grad_gain[0:1, cols] += jnp.sum(upstream * normed, axis=0, keepdims=True)
        grad_qkv[there, 3 * LANES : 4 * LANES] = dv[here, :]
        return carry

    lax.fori_loop(0, blocks, finish, 0)
    grad_attn[...] = jnp.zeros_like(grad_attn)
    for j, (out, half) in enumerate([(keep, 0), (send, 0), (keep, 1), (send, 1)]):
        here = slice(j * size, (j + 1) * size)
        back = contract_cols(grad_qkv[here, :], weights[:, : 4 * LANES])
        out[half * size : (half + 1) * size, :] = back.astype(bf16)
        normed, _ = row_norm(tokens[here, :].astype(f32))
        grad_attn[...] += jnp.sum(back * normed, axis=0, keepdims=True)
    blocks = tokens.shape[1] // LANES
    extra = grad_weights.shape[0] // blocks - LANES
    for k in range(0, blocks, 2):
        cols = slice(k * LANES, (k + 2) * LANES)
        first = contract_rows(normed_low[:, cols], grad_qkv[...]).astype(bf16)
        second = jnp.zeros((2 * LANES, 2 * LANES), f32)
        for j, rows in enumerate((mine, near, far, near_far)):
            second += contract_rows(rows[:, cols], attended[j * size : (j + 1) * size, :])
        for n in range(2):
            at = (k + n) * (LANES + extra)
            rows = slice(n * LANES, (n + 1) * LANES)
            grad_weights[at : at + LANES, : 4 * LANES] = first[rows]
            grad_weights[at : at + LANES, 4 * LANES :] = second[rows].astype(bf16)
    if not ring:
        top[...] = jnp.zeros_like(top)
        bottom[...] = jnp.zeros_like(bottom)
        return
    heads = [grad_gain[0:1, part * LANES : (part + 1) * LANES] for part in range(3)]
    heads = [jnp.broadcast_to(h, (8, LANES)) for h in (heads[0] + heads[1], heads[2])]
    heads = [h + pltpu.roll(h, HD, 1) for h in heads]
    heads = jnp.where(lane_ids(8) < HD, heads[0], heads[1])[0:1]
    for k in range(blocks):
        cols = slice(k * LANES, (k + 1) * LANES)
        at = k * (LANES + extra) + LANES
        row = lax.broadcasted_iota(jnp.int32, (extra, LANES), 0) == 0
        for n, values in enumerate((grad_attn[:, cols], ffn_gain[:, cols], heads)):
            values = jnp.where(row, jnp.broadcast_to(values, (extra, LANES)), 0.0)
            grad_weights[at : at + extra, n * LANES : (n + 1) * LANES] = values.astype(bf16)
        grad_weights[at : at + extra, 3 * LANES :] = jnp.zeros((extra, 3 * LANES), bf16)
    half = blocks // 2 * (LANES + extra)
    top[...] = grad_weights[half : half + HD, :]
    bottom[...] = grad_weights[half + HD : half + LANES + extra, :]


def pack_kernel(w_query, w_key, w_value, w_out, gains, out):
    wide = w_query.shape[1]
    out[:LANES, :wide] = w_query[...]
    out[:LANES, wide : wide + LANES] = w_key[...]
    out[:LANES, wide + LANES : wide + 2 * LANES] = w_value[...]
    out[:LANES, wide + 2 * LANES :] = w_out[...].astype(f32).T.astype(bf16)
    out[LANES:, :] = gains[...]


def pack_ffn_kernel(w_gate, w_up, w_down, out):
    step = out.shape[1] // 3
    out[:, :step] = w_gate[...]
    out[:, step : 2 * step] = w_up[...]
    out[:, 2 * step :] = w_down[...].astype(f32).T.astype(bf16)


def unpack_ffn_kernel(mine, up, down, gate, up_out, down_out):
    step = gate.shape[1]

    def total(part):
        cols = slice(part * step, (part + 1) * step)
        return mine[:, cols].astype(f32) + up[:, cols].astype(f32) + down[:, cols].astype(f32)

    gate[...] = total(0)
    up_out[...] = total(1)
    down_out[...] = total(2).T


def unpack_kernel(mine, up, down, query, key, value, out, gains):
    wide = query.shape[1]
    total = mine[:LANES, :].astype(f32) + up[:LANES, :].astype(f32) + down[:LANES, :].astype(f32)
    rest = slice(LANES, LANES + 16)
    gains[...] = (mine[rest, :].astype(f32) + up[rest, :].astype(f32) + down[rest, :].astype(f32))[:8, : 3 * LANES]
    query[...] = total[:, :wide]
    key[...] = total[:, wide : wide + LANES]
    value[...] = total[:, wide + LANES : wide + 2 * LANES]
    out[...] = total[:, wide + 2 * LANES :].T


def arrange_kernel(ring, place, tokens, out):
    for k in range(tokens.shape[1] // LANES):
        out[:, k * LANES : (k + 1) * LANES] = tokens[:, pl.ds(column(place, k, ring), LANES)]


def arrange_live_kernel(ring, place, cotangent, places, out):
    live = places[...] >= 0
    for k in range(cotangent.shape[1] // LANES):
        values = cotangent[:, pl.ds(column(place, k, ring), LANES)].astype(f32)
        out[:, k * LANES : (k + 1) * LANES] = jnp.where(live, values, 0.0).astype(bf16)


def residual_kernel(part, other, far, tokens, gains, residual, low):
    total = part[...].astype(f32) + other[...].astype(f32) + far[...].astype(f32)
    total = tokens[...].astype(f32) + total
    residual[...] = total
    normed, _ = row_norm(total)
    low[...] = (normed * gains[1:2, :]).astype(bf16)


def put_columns(ring, place, out, values):
    for k in range(values.shape[1] // LANES):
        out[:, pl.ds(column(place, k, ring), LANES)] = values[:, k * LANES : (k + 1) * LANES].astype(out.dtype)


def norm_back(upstream, gain, normed, inverse):
    scaled = upstream * gain
    inner_sum = jnp.mean(scaled * normed, axis=-1, keepdims=True)
    return inverse * (scaled - normed * inner_sum)


def residual_back_kernel(part, other, far, residual, gains, output_low, grad, low, gain_out):
    upstream = part[...].astype(f32) + other[...].astype(f32) + far[...].astype(f32)
    normed, inverse = row_norm(residual[...])
    total = output_low[...].astype(f32) + norm_back(upstream, gains[1:2, :], normed, inverse)
    grad[...] = total
    low[...] = total.astype(bf16)
    gain_out[...] = jnp.sum(upstream * normed, axis=0, keepdims=True)


def output_kernel(ring, place, part, other, far, residual, out):
    total = part[...].astype(f32) + other[...].astype(f32) + far[...].astype(f32)
    put_columns(ring, place, out, residual[...] + total)


def input_back_kernel(ring, place, part, other, far, tokens, gains, grad, out):
    upstream = part[...].astype(f32) + other[...].astype(f32) + far[...].astype(f32)
    normed, inverse = row_norm(tokens[...].astype(f32))
    put_columns(ring, place, out, grad[...] + norm_back(upstream, gains[0:1, :], normed, inverse))


def ffn_kernel(near, near_far, mine, far, output_low, *refs):
    pieces, rest = refs[:9], refs[9:]
    low, active, out_send, out_keep, in_send, in_keep, weights = rest
    size = mine.shape[0]
    step = weights.shape[1] // 3
    half = pl.program_id(0)

    @pl.when(half == 0)
    def _():
        assemble(pieces, weights)
        low[:size, :] = near[...]
        low[size:, :] = near_far[...]

    @pl.when(half == 1)
    def _():
        low[:size, :] = mine[...]
        low[size:, :] = far[...]

    both = product(low[...], weights[:, : 2 * step])
    hidden_grad = product(output_low[...], weights[:, 2 * step :])
    gate, up = both[:, :step], both[:, step:]
    sigmoid = 1.0 / (1.0 + jnp.exp(-gate))
    silu = gate * sigmoid
    active[:, 2 * step :] = (silu * up).astype(bf16)
    active[:, :step] = (hidden_grad * up * (sigmoid + silu * (1.0 - sigmoid))).astype(bf16)
    active[:, step : 2 * step] = (hidden_grad * silu).astype(bf16)
    out = contract_cols(active[:, 2 * step :], weights[:, 2 * step :])
    into = contract_cols(active[:, : 2 * step], weights[:, : 2 * step])

    @pl.when(half == 0)
    def _():
        out_send[...] = out.astype(bf16)
        in_send[...] = into.astype(bf16)

    @pl.when(half == 1)
    def _():
        out_keep[...] = out.astype(bf16)
        in_keep[...] = into.astype(bf16)


def ffn_weights_kernel(low, output_low, active, out, top, bottom):
    step = active.shape[1] // 3
    out[:, : 2 * step] = product(low[...].T, active[:, : 2 * step]).astype(bf16)
    out[:, 2 * step :] = product(output_low[...].T, active[:, 2 * step :]).astype(bf16)

    @pl.when(pl.program_id(0) == 0)
    def _():
        top[...] = out[:HD, :]
        bottom[...] = out[HD:LANES, :]


def shape_of(*dims, dtype=bf16):
    return jax.ShapeDtypeStruct(dims, dtype)


def params(mebibytes=48):
    return pltpu.CompilerParams(vmem_limit_bytes=mebibytes * 2**20)


def cost(flops, bytes_moved, exps=0):
    return pl.CostEstimate(flops=int(flops), bytes_accessed=int(bytes_moved), transcendentals=int(exps))


def simple(kernel, outs, name, args, n_scalars=0):
    return pl.pallas_call(
        kernel,
        out_shape=outs,
        in_specs=[scalars] * n_scalars + [whole_vmem] * (len(args) - n_scalars),
        out_specs=jax.tree.map(lambda _: whole_vmem, outs),
        compiler_params=params(),
        name=name,
    )(*args)


def first_rows(rows, cols, at=0):
    return pl.BlockSpec((rows, cols), lambda i: (at, 0))


def own_rows(kernel, rows, width, outs, name, place, args, places=()):
    specs = [scalars] if place is not None else []
    specs += [first_rows(min(rows, a.shape[0]), width, dict(places).get(n, 0)) for n, a in enumerate(args)]
    return pl.pallas_call(
        kernel,
        grid=(1,),
        out_shape=outs,
        in_specs=specs,
        out_specs=tuple(first_rows(o.shape[0], width) for o in outs),
        compiler_params=params(),
        cost_estimate=cost(8 * rows * width, 12 * rows * width),
        name=name,
    )(*([place] if place is not None else []), *args)


def feed_forward(rows_in, output_low, pieces):
    slots, width = output_low.shape
    cols = pieces[0].shape[1]
    half = slots // 2
    wide = shape_of(half, width)
    moving = lambda n: pl.BlockSpec((half, n), lambda i: (i, 0))
    return pl.pallas_call(
        ffn_kernel,
        grid=(2,),
        out_shape=(shape_of(slots, width), shape_of(slots, cols), wide, wide, wide, wide),
        in_specs=[whole_vmem] * 4 + [moving(width)] + [whole_vmem] * 9,
        out_specs=(moving(width), moving(cols)) + (whole_vmem,) * 4,
        scratch_shapes=[pltpu.VMEM((width, cols), bf16)],
        compiler_params=params(56),
        cost_estimate=cost(4 * slots * width * cols, 20 * 2**20, 2e6),
        name="ffn",
    )(*rows_in, output_low, *pieces)


def feed_forward_weights(low, output_low, active, first, number):
    slots, width = low.shape
    cols = active.shape[1]
    pair = 2 * LANES
    pairs = width // pair
    side = pl.BlockSpec((slots, pair), lambda i: (0, lax.rem(i + first, pairs)))
    return pl.pallas_call(
        ffn_weights_kernel,
        grid=(number,),
        out_shape=(shape_of(number * pair, cols), shape_of(HD, cols), shape_of(HD, cols)),
        in_specs=[side, side, whole_vmem],
        out_specs=(pl.BlockSpec((pair, cols), lambda i: (i, 0)), whole_vmem, whole_vmem),
        compiler_params=params(),
        cost_estimate=cost(2 * slots * pair * number * cols, 12 * 2**20),
        name="ffn_weights",
    )(low, output_low, active)


def rotary_tables(slot_positions):
    powers = jnp.arange(HD // 2, dtype=f32) * (2.0 / HD)
    frequency = rope_base ** (-powers)
    angles = jnp.maximum(slot_positions, 0).astype(f32)[:, None] * frequency[None, :]
    return jnp.cos(angles), jnp.sin(angles)


def per_device(
    tokens, positions, attn_gain, query_gain, key_gain, w_query, w_key, w_value, w_out, ffn_gain,
    w_gate, w_up, w_down, cotangent,
):
    slots, width = tokens.shape
    count = lax.axis_size("dp")
    me = lax.axis_index("dp")
    place = lax.axis_index("tensor").astype(jnp.int32)
    rows = slots // 4
    ring = count * LANES == width and count % 2 == 0
    hidden = w_gate.shape[1]
    q_cols, k_cols = w_query.shape[1], w_key.shape[1]
    attn_cols = q_cols + 2 * k_cols + w_out.shape[0]

    if ring:
        spot = jnp.where(me % 2 == 0, me // 2, count - 1 - me // 2)
    else:
        spot = me
    length = count if ring else 0
    place = jnp.stack([place, spot.astype(jnp.int32)])

    def in_place(kernel):
        return functools.partial(kernel, length)

    if ring:
        gains_row = jnp.pad(
            jnp.concatenate([attn_gain, ffn_gain])[None, :], ((0, 15), (0, attn_cols - 2 * LANES))
        )
        attn_block = simple(
            pack_kernel, shape_of(LANES + 16, attn_cols), "pack", (w_query, w_key, w_value, w_out, gains_row)
        )
        ffn_block = simple(pack_ffn_kernel, shape_of(LANES, 3 * hidden), "pack_ffn", (w_gate, w_up, w_down))
    else:
        gathered = lax.all_gather(
            jnp.concatenate([w_query, w_key, w_value, w_out.T], axis=1), "dp", axis=0, tiled=True
        )
        gains_all = jnp.stack(
            [lax.all_gather(g, "dp", axis=0, tiled=True) for g in (attn_gain, ffn_gain)], axis=0
        )
        attn_pieces = []
        for k, piece in enumerate(pieces_of(gathered)):
            column = k * LANES if k < 4 else (k - 1) * LANES
            pad = jnp.pad(
                gains_all[:, column : column + LANES].reshape(1, -1), ((0, 15), (0, attn_cols - 2 * LANES))
            )
            attn_pieces.append(piece if k == 4 else jnp.concatenate([piece, pad], axis=0))
        turned = w_down.T
        block = jnp.concatenate([w_gate, w_up, turned], axis=1)
        ffn_pieces = pieces_of(lax.all_gather(block, "dp", axis=0, tiled=True))

    places = jnp.broadcast_to(positions[:, None], (slots, LANES))
    place_rows = positions.reshape(4, 1, rows)
    straight = pl.BlockSpec((rows, width), lambda i, s: (i, 0))

    def arranged(kernel, row_of, args, name):
        return pl.pallas_call(
            in_place(kernel),
            out_shape=shape_of(slots, width),
            grid_spec=pltpu.PrefetchScalarGridSpec(
                num_scalar_prefetch=1,
                grid=(4,),
                in_specs=[pl.BlockSpec((rows, a.shape[1]), lambda i, s: (row_of(i) ^ s[0], 0)) for a in args],
                out_specs=straight,
            ),
            cost_estimate=cost(0, 4 * slots * width),
            name=name,
        )(place, *args)

    inputs = arranged(arrange_kernel, lambda i: i, (tokens,), "arrange")
    output_low = arranged(arrange_live_kernel, lambda i: lax.rem(2 * i + 1, 5), (cotangent, places), "arrange_live")
    tables = rotary_tables(positions)
    if ring:
        attn_ring, ffn_ring = RingGather(attn_block, count), RingGather(ffn_block, count)
        attn_ring.send()
        attn_ring.tie(*ffn_ring.moving)
        attn_ring.send()
        (inputs,) = attn_ring.tie(inputs)
        attn_ring.send()
        tables = attn_ring.tie(*tables)
        attn_ring.send()
        ffn_ring.moving = after(ffn_ring.moving, attn_ring.moving)
        ffn_ring.send()
        attn_pieces = attn_ring.pieces()
    gain_q = jnp.tile(query_gain.astype(f32), 2)[None, :]
    gain_k = jnp.tile(key_gain.astype(f32), 2)[None, :]

    weights, gains, normed_low, qkv, q, k, v, cosine, sine = pl.pallas_call(
        project_kernel,
        out_shape=(
            shape_of(width, attn_cols),
            shape_of(8, width, dtype=f32),
            shape_of(slots, width),
            shape_of(slots, 4 * LANES, dtype=f32),
            shape_of(slots, 2 * LANES),
            shape_of(slots, LANES),
            shape_of(slots, LANES),
            shape_of(slots, LANES, dtype=f32),
            shape_of(slots, LANES, dtype=f32),
        ),
        in_specs=[scalars] + [whole_vmem] * 14,
        out_specs=(whole_vmem,) * 9,
        compiler_params=params(),
        cost_estimate=cost(3e9, 14 * 2**20, 3e6),
        name="project",
    )(place, inputs, *tables, gain_q, gain_k, *attn_pieces)
    halved = shape_of(slots // 2, width)
    attended, inverse_total, attn_send, attn_keep = pl.pallas_call(
        attention_kernel,
        out_shape=(shape_of(slots, 2 * LANES), shape_of(slots, 2 * LANES, dtype=f32), halved, halved),
        in_specs=[scalars] + [whole_vmem] * 5,
        out_specs=(whole_vmem,) * 4,
        scratch_shapes=[
            pltpu.VMEM((4, slots, LANES), bf16),
            pltpu.VMEM((4, slots, LANES), bf16),
            pltpu.VMEM((4, rows, LANES), f32),
        ],
        compiler_params=params(),
        cost_estimate=cost(9e9, 8 * 2**20, 3e6),
        name="attention",
    )(place, places, weights, q, k, v)

    other = swap(attn_send, "tensor", 1)
    if ring:
        (other,) = after((other,), ffn_ring.moving)
        ffn_ring.send()
    far = swap(add(attn_keep[rows:], other[rows:]), "tensor", 2)
    if ring:
        (far,) = after((far,), ffn_ring.moving)
        ffn_ring.send()
    row_f32, row_bf16 = shape_of(rows, width, dtype=f32), shape_of(rows, width)
    one_gain = shape_of(1, width, dtype=f32)
    residual, ffn_rows = own_rows(
        residual_kernel, rows, width, (row_f32, row_bf16), "residual", None, (attn_keep, other, far, inputs, gains)
    )
    near, far = swap(ffn_rows, "tensor", 1), swap(ffn_rows, "tensor", 2)
    if ring:
        (far,) = after((far,), ffn_ring.moving)
        ffn_ring.send()
        ffn_pieces = ffn_ring.pieces()
    rows_in = near, swap(far, "tensor", 1), ffn_rows, far

    ffn_low, active, out_send, out_keep, in_send, in_keep = feed_forward(rows_in, output_low, ffn_pieces)
    other = swap(in_send, "tensor", 1)
    if ring:
        half = count // 2
        toward_y = add(in_keep[rows:], other[rows:])
        (active,) = after((active,), (toward_y,))
        first_grad, top, bottom = feed_forward_weights(ffn_low, output_low, active, half // 2, 1)
        next_grad, _, _ = feed_forward_weights(ffn_low, output_low, active, half // 2 - 1, 1)
        ffn_grads = {half // 2: first_grad, half // 2 - 1: next_grad}

        def ffn_block_of(k):
            return ffn_grads[k // 2][k % 2 * LANES : (k % 2 + 1) * LANES]

        ffn_scatter = RingScatter(ffn_block_of, top, bottom, count)
        ffn_scatter.send()
        far = swap(toward_y, "tensor", 2)
    else:
        grad_ffn, _, _ = feed_forward_weights(ffn_low, output_low, active, 0, width // (2 * LANES))
        far = swap(add(in_keep[rows:], other[rows:]), "tensor", 2)
    residual_grad, residual_low, ffn_gain_part = own_rows(
        residual_back_kernel, rows, width, (row_f32, row_bf16, one_gain), "residual_back", None,
        (in_keep, other, far, residual, gains, output_low), [(5, 2)],
    )
    rows_back = tensor_gather(residual_low)
    if ring:
        (active,) = after((active,), (residual_low,))
        ffn_scatter.moving = after(ffn_scatter.moving, (residual_low,))
        ffn_scatter.add()
        ffn_scatter.send()
        rest_grad, _, _ = feed_forward_weights(ffn_low, output_low, active, half // 2 + 1, half // 2)
        ffn_grads[half // 2 + 1], ffn_grads[0] = rest_grad[: 2 * LANES], rest_grad[2 * LANES :]
        ffn_scatter.add()
        rows_back = after(rows_back, ffn_scatter.moving)
        ffn_scatter.send()

    grads = pl.pallas_call(
        backward_kernel,
        out_shape=(
            shape_of(slots, 2 * LANES, dtype=f32), shape_of(slots, LANES, dtype=f32), shape_of(slots, LANES),
        ),
        in_specs=[scalars] + [whole_vmem] * 11,
        out_specs=(whole_vmem,) * 3,
        scratch_shapes=[
            pltpu.VMEM((slots, 2 * LANES), bf16),
            pltpu.VMEM((4, slots, LANES), bf16),
            pltpu.VMEM((4, slots, LANES), bf16),
            pltpu.VMEM((4, 4, LANES, rows), bf16),
            pltpu.VMEM((slots, 2 * LANES), bf16),
            pltpu.VMEM((4, slots, LANES), bf16),
            pltpu.VMEM((2, 4, LANES, rows), f32),
            pltpu.VMEM((2, rows, LANES), f32),
            pltpu.VMEM((2, rows, LANES), f32),
        ],
        compiler_params=params(),
        cost_estimate=cost(16e9, 8 * 2**20, 3e6),
        name="attention_backward",
    )(place, place_rows, weights, q, k, v, attended, inverse_total, *rows_back)
    if ring:
        ffn_scatter.add()
        grads = after(grads, ffn_scatter.moving)
        ffn_scatter.send()
    tall = LANES + 16 if ring else LANES
    grad_attn, top, bottom, attn_send, attn_keep, attn_gain_part, head_gains = pl.pallas_call(
        in_place(backward_end_kernel),
        out_shape=(
            shape_of(width // LANES * tall, attn_cols),
            shape_of(HD, attn_cols),
            shape_of(tall - HD, attn_cols),
            halved,
            halved,
            one_gain,
            shape_of(8, 3 * LANES, dtype=f32),
        ),
        in_specs=[scalars] + [whole_vmem] * 17,
        out_specs=(whole_vmem,) * 7,
        scratch_shapes=[pltpu.VMEM((slots, 4 * LANES), bf16)],
        compiler_params=params(),
        cost_estimate=cost(9e9, 14 * 2**20),
        name="backward_end",
    )(
        place, inputs, weights, normed_low, qkv, cosine, sine, gain_q, gain_k, attended, *rows_back,
        ffn_gain_part, *grads,
    )

    (out_send,) = after((out_send,), rows_back)
    out_other, out_far = tensor_scatter(out_send, out_keep)
    (block_output,) = own_rows(
        in_place(output_kernel), rows, width, (row_bf16,), "output", place, (out_keep, out_other, out_far, residual)
    )
    other, far = tensor_scatter(attn_send, attn_keep)
    (input_grad,) = own_rows(
        in_place(input_back_kernel), rows, width, (row_bf16,), "input_back", place,
        (attn_keep, other, far, inputs, gains, residual_grad),
    )
    if ring:
        attn_scatter = RingScatter(lambda k: grad_attn[k * tall : (k + 1) * tall], top, bottom, count)
        attn_scatter.send()
        for step in range(half - 1):
            attn_scatter.add()
            if step == 0:
                attn_scatter.moving = after(attn_scatter.moving, ffn_scatter.moving)
            if step == half - 2:
                attn_scatter.moving = after(attn_scatter.moving, (far,))
            attn_scatter.send()
        shard_query, shard_key, shard_value, shard_out, gain_part = simple(
            unpack_kernel,
            (*(shape_of(*w.shape, dtype=f32) for w in (w_query, w_key, w_value, w_out)), shape_of(8, 3 * LANES, dtype=f32)),
            "unpack",
            (grad_attn[:tall], *attn_scatter.moving),
        )
        gain_total = gain_part + sum(swap(gain_part, "tensor", bits) for bits in (1, 2, 3))
        grad_attn_gain, grad_ffn_gain, heads = (gain_total[0, k * LANES : (k + 1) * LANES] for k in range(3))
        grad_query_gain, grad_key_gain = heads[:HD], heads[HD:]
        shard_gate, shard_up, shard_down = simple(
            unpack_ffn_kernel,
            tuple(jax.ShapeDtypeStruct(w.shape, f32) for w in (w_gate, w_up, w_down)),
            "unpack_ffn",
            (ffn_block_of(0), *ffn_scatter.moving),
        )
    else:
        gain_total = sum_all(jnp.concatenate([attn_gain_part, ffn_gain_part, head_gains[0:1]], axis=1))[0]
        share = width // count
        grad_attn_gain = lax.dynamic_slice_in_dim(gain_total, me * share, share)
        grad_ffn_gain = lax.dynamic_slice_in_dim(gain_total, width + me * share, share)
        heads = gain_total[2 * width :].reshape(-1, HD)
        grad_query_gain = jnp.sum(heads[:4], axis=0)
        grad_key_gain = jnp.sum(heads[4:], axis=0)
        total = lax.psum_scatter(grad_attn, "dp", scatter_dimension=0, tiled=True).astype(f32)
        shard_query, shard_key, shard_value, turned = jnp.split(total, np.cumsum([q_cols, k_cols, k_cols]), axis=1)
        shard_out = turned.T
        total = lax.psum_scatter(grad_ffn, "dp", scatter_dimension=0, tiled=True).astype(f32)
        shard_gate, shard_up, turned = jnp.split(total, 3, axis=1)
        shard_down = turned.T
    return (
        block_output,
        input_grad,
        grad_attn_gain,
        grad_query_gain,
        grad_key_gain,
        shard_query,
        shard_key,
        shard_value,
        shard_out,
        grad_ffn_gain,
        shard_gate,
        shard_up,
        shard_down,
    )


def solution(mesh):
    in_specs = (
        P("dp", None), P("dp"), P("dp"), P(), P(), P("dp", "tensor"), P("dp", "tensor"), P("dp", "tensor"),
        P("tensor", "dp"), P("dp"), P("dp", "tensor"), P("dp", "tensor"), P("tensor", "dp"), P("dp", None),
    )
    out_specs = (
        P(("dp", "tensor"), None), P(("dp", "tensor"), None), P("dp"), P(), P(), P("dp", "tensor"),
        P("dp", "tensor"), P("dp", "tensor"), P("tensor", "dp"), P("dp"), P("dp", "tensor"), P("dp", "tensor"),
        P("tensor", "dp"),
    )
    return jax.shard_map(
        per_device, mesh=mesh, in_specs=in_specs, out_specs=out_specs, check_vma=False
    )
```

profile of v0, /device:TPU:0, one launch (start us, length us, event | category | flops | bytes accessed | tf_op | source)
XLA Modules:
  0.0 281.1 jit_solution(18183860390639505727)
XLA Ops:
  4.7 3.0 %collective-permute-start.1 = (bf16[144,768]{1,0:T(8,128)(2,1)S(1)}, bf16[144,768]{1,0:T(8,128)(2,1)S(1)}, u32[]{:S(2)}, u32[]{:S(2)}) collective-permute-start(bf16[144,768]{1,0:T(8,128)(2,1)S(1)} %pack.1.p0), channel_id=1, source_target_pairs={{8,0},{16,8},{24,16},{28,24},{20,28},{12,20},{4,12},{0,4},{9,1},{1... | collective-permute-start | bytes 663560 | tf_op jit(solution)/shard_map/ppermute | solution.py:65
  8.4 4.8 %arrange.1.tokens = bf16[1024,1024]{1,0:T(8,128)(2,1)} custom-call(s32[2]{0:T(128)} %pad_add_fusion.place, bf16[1024,1024]{1,0:T(8,128)(2,1)} %tokens.1), custom_call_target="tpu_custom_call" | custom-call | bytes 4194304 | tf_op jit(solution)/shard_map/arrange/pallas_call | solution.py:733
  16.6 3.9 %collective-permute-done.2.p7 = bf16[144,768]{1,0:T(8,128)(2,1)S(1)} collective-permute-done((bf16[144,768]{1,0:T(8,128)(2,1)S(1)}, bf16[144,768]{1,0:T(8,128)(2,1)S(1)}, u32[]{:S(2)}, u32[]{:S(2)}) %collective-permute-start.2) | collective-permute-done | bytes 221216 | tf_op jit(solution)/shard_map/ppermute | solution.py:65
  24.5 1.9 multiply_sine_fusion
  32.8 4.2 %collective-permute-done.6.p4 = bf16[64,768]{1,0:T(8,128)(2,1)} collective-permute-done((bf16[64,768]{1,0:T(8,128)(2,1)}, bf16[64,768]{1,0:T(8,128)(2,1)}, u32[]{:S(2)}, u32[]{:S(2)}) %collective-permute-start.6) | collective-permute-done | bytes 98336 | tf_op jit(solution)/shard_map/ppermute | solution.py:65
  40.0 8.1 %project.1 = (bf16[1024,768]{1,0:T(8,128)(2,1)}, f32[8,1024]{1,0:T(8,128)S(1)}, bf16[1024,1024]{1,0:T(8,128)(2,1)}, f32[1024,512]{1,0:T(8,128)}, bf16[1024,256]{...) custom-call(s32[2]{0:T(128)S(1)} %copy-done.17, ...), custom_call_target="tpu_custom_call" | custom-call | flops 3000000000 | bytes 14680064 | tf_op jit(solution)/shard_map/project/pallas_call | solution.py:764
  49.7 10.2 %attention.1 = (bf16[1024,256]{1,0:T(8,128)(2,1)S(1)}, f32[1024,256]{1,0:T(8,128)S(1)}, bf16[512,1024]{1,0:T(8,128)(2,1)S(1)}, bf16[512,1024]{1,0:T(8,128)(2,1)S(1)}) custom-call(s32[2]{0:T(128)S(1)} %copy-done.17, s32[1024,128]{1,0:T(8,128)S(1)} %broadcast_in_dim.4.places, bf16[1024,768]{1,0:T(8,128)(2,1)} %get-tuple-element.97.weights, ...), custom_call_target="tpu_custom_call" | custom-call | flops 8999999488 | bytes 8388608 | tf_op jit(solution)/shard_map/attention/pallas_call | solution.py:784
  65.4 17.6 %collective-permute-done.12.refs_7_ = bf16[128,3456]{1,0:T(8,128)(2,1)S(1)} collective-permute-done((bf16[128,3456]{1,0:T(8,128)(2,1)S(1)}, bf16[128,3456]{1,0:T(8,128)(2,1)S(1)}, u32[]{:S(2)}, u32[]{:S(2)}) %collective-permute-start.12) | collective-permute-done | bytes 884768 | tf_op jit(solution)/shard_map/ppermute | solution.py:65
  88.1 11.7 %collective-permute-done.15.far = bf16[256,1024]{1,0:T(8,128)(2,1)} collective-permute-done((bf16[256,1024]{1,0:T(8,128)(2,1)S(1)}, bf16[256,1024]{1,0:T(8,128)(2,1)}, u32[]{:S(2)}, u32[]{:S(2)}) %collective-permute-start.15) | collective-permute-done | bytes 524320 | tf_op jit(solution)/shard_map/ppermute | solution.py:122
  99.8 4.4 %collective-permute-done.16.refs_6_ = bf16[128,3456]{1,0:T(8,128)(2,1)S(1)} collective-permute-done((bf16[128,3456]{1,0:T(8,128)(2,1)S(1)}, bf16[128,3456]{1,0:T(8,128)(2,1)S(1)}, u32[]{:S(2)}, u32[]{:S(2)}) %collective-permute-start.16) | collective-permute-done | bytes 884768 | tf_op jit(solution)/shard_map/ppermute | solution.py:65
  107.9 4.8 %arrange_live.1.output_low = bf16[1024,1024]{1,0:T(8,128)(2,1)} custom-call(s32[2]{0:T(128)} %pad_add_fusion.place, bf16[1024,1024]{1,0:T(8,128)(2,1)} %cotangent.1, s32[1024,128]{1,0:T(8,128)} %copy-done.7), custom_call_target="tpu_custom_call" | custom-call | bytes 4194304 | tf_op jit(solution)/shard_map/arrange_live/pallas_call | solution.py:733
  112.7 5.6 %collective-permute-done.19.refs_4_ = bf16[64,3456]{1,0:T(8,128)(2,1)} collective-permute-done((bf16[64,3456]{1,0:T(8,128)(2,1)S(1)}, bf16[64,3456]{1,0:T(8,128)(2,1)}, u32[]{:S(2)}, u32[]{:S(2)}) %collective-permute-start.19) | collective-permute-done | bytes 442400 | tf_op jit(solution)/shard_map/ppermute | solution.py:65
  119.9 24.5 %ffn.1 = (bf16[1024,1024]{1,0:T(8,128)(2,1)}, bf16[1024,3456]{1,0:T(8,128)(2,1)}, bf16[512,1024]{1,0:T(8,128)(2,1)}, bf16[512,1024]{1,0:T(8,128)(2,1)}, bf16[512...) custom-call(bf16[256,1024]{1,0:T(8,128)(2,1)} %collective-permute-done.14.near, ...), custom_call_target="tpu_custom_call" | custom-call | flops 14495514624 | bytes 20971520 | tf_op jit(solution)/shard_map/ffn/pallas_call | solution.py:640
  144.5 2.9 %collective-permute-done.21.other = bf16[512,1024]{1,0:T(8,128)(2,1)S(1)} collective-permute-done((bf16[512,1024]{1,0:T(8,128)(2,1)}, bf16[512,1024]{1,0:T(8,128)(2,1)S(1)}, u32[]{:S(2)}, u32[]{:S(2)}) %collective-permute-start.21) | collective-permute-done | bytes 1048608 | tf_op jit(solution)/shard_map/ppermute | solution.py:122
  151.8 5.4 %ffn_weights.4 = (bf16[256,3456]{1,0:T(8,128)(2,1)S(1)}, bf16[64,3456]{1,0:T(8,128)(2,1)S(1)}, bf16[64,3456]{1,0:T(8,128)(2,1)S(1)}) custom-call(bf16[1024,1024]{1,0:T(8,128)(2,1)S(1)} %copy-done.2, bf16[1024,1024]{1,0:T(8,128)(2,1)} %arrange_live.1.output_low, bf16[1024,3456]{1,0:T(8,128)(2,1)} %get-tuple-element.123.active), custom_call_target="tpu_custom_call" | custom-call | flops 1811939328 | bytes 12582912 | tf_op jit(solution)/shard_map/ffn_weights/pallas_call | solution.py:659
  159.3 6.3 %ffn_weights.3 = (bf16[256,3456]{1,0:T(8,128)(2,1)S(1)}, bf16[64,3456]{1,0:T(8,128)(2,1)}, bf16[64,3456]{1,0:T(8,128)(2,1)}) custom-call(bf16[1024,1024]{1,0:T(8,128)(2,1)S(1)} %copy-done.2, bf16[1024,1024]{1,0:T(8,128)(2,1)} %arrange_live.1.output_low, bf16[1024,3456]{1,0:T(8,128)(2,1)} %get-tuple-element.123.active), custom_call_target="tpu_custom_call" | custom-call | flops 1811939328 | bytes 12582912 | tf_op jit(solution)/shard_map/ffn_weights/pallas_call | solution.py:659
  172.9 8.9 %ffn_weights.5 = (bf16[512,3456]{1,0:T(8,128)(2,1)}, bf16[64,3456]{1,0:T(8,128)(2,1)}, bf16[64,3456]{1,0:T(8,128)(2,1)}) custom-call(bf16[1024,1024]{1,0:T(8,128)(2,1)S(1)} %copy-done.3, bf16[1024,1024]{1,0:T(8,128)(2,1)S(1)} %copy-done, bf16[1024,3456]{1,0:T(8,128)(2,1)} %get-tuple-element.123.active), custom_call_target="tpu_custom_call" | custom-call | flops 3623878656 | bytes 12582912 | tf_op jit(solution)/shard_map/ffn_weights/pallas_call | solution.py:659
  181.9 9.0 %collective-permute-done.28 = bf16[128,3456]{1,0:T(8,128)(2,1)S(1)} collective-permute-done((bf16[128,3456]{1,0:T(8,128)(2,1)S(1)}, bf16[128,3456]{1,0:T(8,128)(2,1)S(1)}, u32[]{:S(2)}, u32[]{:S(2)}) %collective-permute-start.28) | collective-permute-done | bytes 884768 | tf_op jit(solution)/shard_map/ppermute | solution.py:92
  194.7 16.7 %attention_backward.1 = (f32[1024,256]{1,0:T(8,128)S(1)}, f32[1024,128]{1,0:T(8,128)S(1)}, bf16[1024,128]{1,0:T(8,128)(2,1)S(1)}) custom-call(s32[2]{0:T(128)S(1)} %copy-done.18, s32[4,1,256]{2,1,0:T(1,128)S(1)} %bitcast.11, bf16[1024,768]{1,0:T(8,128)(2,1)} %get-tuple-element.97.weights, bf16[1024,256]{1,0:T(8,128)(2,1)S(1)} %copy-done.27, ...), custom_call_target="tpu_custom_call" | custom-call | flops 16000000000 | bytes 8388608 | tf_op jit(solution)/shard_map/attention_backward/pallas_call | solution.py:854
  212.8 1.9 add_convert_fusion
  216.8 11.0 %backward_end.1 = (bf16[1152,768]{1,0:T(8,128)(2,1)}, bf16[64,768]{1,0:T(8,128)(2,1)S(1)}, bf16[80,768]{1,0:T(8,128)(2,1)S(1)}, bf16[512,1024]{1,0:T(8,128)(2,1)...) custom-call(s32[2]{0:T(128)S(1)} %copy-done.18, bf16[1024,1024]{1,0:T(8,128)(2,1)} %arrange.1.tokens, ...), custom_call_target="tpu_custom_call" | custom-call | flops 8999999488 | bytes 14680064 | tf_op jit(solution)/shard_map/backward_end/pallas_call | solution.py:881
  231.6 4.1 %collective-permute-done.36 = bf16[64,768]{1,0:T(8,128)(2,1)S(1)} collective-permute-done((bf16[64,768]{1,0:T(8,128)(2,1)S(1)}, bf16[64,768]{1,0:T(8,128)(2,1)S(1)}, u32[]{:S(2)}, u32[]{:S(2)}) %collective-permute-start.36) | collective-permute-done | bytes 98336 | tf_op jit(solution)/shard_map/ppermute | solution.py:92
  239.9 5.8 %collective-permute-done.42 = bf16[144,768]{1,0:T(8,128)(2,1)S(1)} collective-permute-done((bf16[144,768]{1,0:T(8,128)(2,1)S(1)}, bf16[144,768]{1,0:T(8,128)(2,1)S(1)}, u32[]{:S(2)}, u32[]{:S(2)}) %collective-permute-start.42) | collective-permute-done | bytes 221216 | tf_op jit(solution)/shard_map/ppermute | solution.py:92
  247.5 3.0 %collective-permute-start.35 = (bf16[256,1024]{1,0:T(8,128)(2,1)S(1)}, bf16[256,1024]{1,0:T(8,128)(2,1)S(1)}, u32[]{:S(2)}, u32[]{:S(2)}) collective-permute-start(bf16[256,1024]{1,0:T(8,128)(2,1)S(1)} %add_convert_fusion.4), channel_id=1, source_target_pairs={{0,2},{1,3},{2,0},{3,1},{4,6},{5,7},{6,4},{7,5},{8,10},{9,11},{10,... | collective-permute-start | bytes 1572872 | tf_op jit(solution)/shard_map/ppermute | solution.py:122
  250.6 3.2 %collective-permute-done.43 = bf16[144,768]{1,0:T(8,128)(2,1)S(1)} collective-permute-done((bf16[144,768]{1,0:T(8,128)(2,1)S(1)}, bf16[144,768]{1,0:T(8,128)(2,1)S(1)}, u32[]{:S(2)}, u32[]{:S(2)}) %collective-permute-start.43) | collective-permute-done | bytes 221216 | tf_op jit(solution)/shard_map/ppermute | solution.py:92
  255.2 3.7 %collective-permute-start.31 = (bf16[256,1024]{1,0:T(8,128)(2,1)S(1)}, bf16[256,1024]{1,0:T(8,128)(2,1)S(1)}, u32[]{:S(2)}, u32[]{:S(2)}) collective-permute-start(bf16[256,1024]{1,0:T(8,128)(2,1)S(1)} %add_convert_fusion.5), channel_id=1, source_target_pairs={{0,2},{1,3},{2,0},{3,1},{4,6},{5,7},{6,4},{7,5},{8,10},{9,11},{10,... | collective-permute-start | bytes 1572872 | tf_op jit(solution)/shard_map/ppermute | solution.py:122
  260.2 3.1 %collective-permute-done.35.far = bf16[256,1024]{1,0:T(8,128)(2,1)S(1)} collective-permute-done((bf16[256,1024]{1,0:T(8,128)(2,1)S(1)}, bf16[256,1024]{1,0:T(8,128)(2,1)S(1)}, u32[]{:S(2)}, u32[]{:S(2)}) %collective-permute-start.35) | collective-permute-done | bytes 524320 | tf_op jit(solution)/shard_map/ppermute | solution.py:122
  263.3 1.8 collective-permute-start.44
  265.4 3.9 %collective-permute-done.44.up = bf16[144,768]{1,0:T(8,128)(2,1)S(1)} collective-permute-done((bf16[144,768]{1,0:T(8,128)(2,1)S(1)}, bf16[144,768]{1,0:T(8,128)(2,1)S(1)}, u32[]{:S(2)}, u32[]{:S(2)}) %collective-permute-start.44) | collective-permute-done | bytes 221216 | tf_op jit(solution)/shard_map/ppermute | solution.py:92
  269.3 1.8 collective-permute-done.45.down
  271.8 2.1 collective-permute-start.47
  278.0 2.0 input_back.1
  (221 shorter events, 78.6 us)
Async XLA Ops:
  4.7 8.8 %collective-permute-start.1 = (bf16[144,768]{1,0:T(8,128)(2,1)S(1)}, bf16[144,768]{1,0:T(8,128)(2,1)S(1)}, u32[]{:S(2)}, u32[]{:S(2)}) collective-permute-start(bf16[144,768]{1,0:T(8,128)(2,1)S(1)} %pack.1.p0), channel_id=1, source_target_pairs={{8,0},{16,8},{24,16},{28,24},{20,28},{12,20},{4,12},{0,4},{9,1},{1... | collective-permute-start | bytes 663560 | tf_op jit(solution)/shard_map/ppermute | solution.py:65
  37.0 23.9 %collective-permute-start.9 = (bf16[128,3456]{1,0:T(8,128)(2,1)S(1)}, bf16[128,3456]{1,0:T(8,128)(2,1)S(1)}, u32[]{:S(2)}, u32[]{:S(2)}) collective-permute-start(bf16[128,3456]{1,0:T(8,128)(2,1)S(1)} %pack_ffn.1.refs_0_), channel_id=1, source_target_pairs={{0,8},{8,16},{16,24},{24,28},{28,20},{20,12},{12,4},{4,0},{1,9},{9... | collective-permute-start | bytes 2654216 | tf_op jit(solution)/shard_map/ppermute | solution.py:65
  38.6 24.0 %collective-permute-start.10 = (bf16[128,3456]{1,0:T(8,128)(2,1)S(1)}, bf16[128,3456]{1,0:T(8,128)(2,1)S(1)}, u32[]{:S(2)}, u32[]{:S(2)}) collective-permute-start(bf16[128,3456]{1,0:T(8,128)(2,1)S(1)} %pack_ffn.1.refs_0_), channel_id=1, source_target_pairs={{8,0},{16,8},{24,16},{28,24},{20,28},{12,20},{4,12},{0,4},{9,1},{1... | collective-permute-start | bytes 2654216 | tf_op jit(solution)/shard_map/ppermute | solution.py:65
  61.0 22.1 %collective-permute-start.12 = (bf16[128,3456]{1,0:T(8,128)(2,1)S(1)}, bf16[128,3456]{1,0:T(8,128)(2,1)S(1)}, u32[]{:S(2)}, u32[]{:S(2)}) collective-permute-start(bf16[128,3456]{1,0:T(8,128)(2,1)S(1)} %collective-permute-done.9.refs_8_), channel_id=1, source_target_pairs={{0,8},{8,16},{16,24},{24,28},{28,20},{20,12},{12,4},{4,0},{1,9},{9... | collective-permute-start | bytes 2654216 | tf_op jit(solution)/shard_map/ppermute | solution.py:65
  62.6 22.0 %collective-permute-start.13 = (bf16[128,3456]{1,0:T(8,128)(2,1)S(1)}, bf16[128,3456]{1,0:T(8,128)(2,1)S(1)}, u32[]{:S(2)}, u32[]{:S(2)}) collective-permute-start(bf16[128,3456]{1,0:T(8,128)(2,1)S(1)} %collective-permute-done.10.refs_1_), channel_id=1, source_target_pairs={{8,0},{16,8},{24,16},{28,24},{20,28},{12,20},{4,12},{0,4},{9,1},{1... | collective-permute-start | bytes 2654216 | tf_op jit(solution)/shard_map/ppermute | solution.py:65
  63.8 21.2 %collective-permute-start.11 = (bf16[256,1024]{1,0:T(8,128)(2,1)S(1)}, bf16[256,1024]{1,0:T(8,128)(2,1)S(1)}, u32[]{:S(2)}, u32[]{:S(2)}) collective-permute-start(bf16[256,1024]{1,0:T(8,128)(2,1)S(1)} %add_convert_fusion.7), channel_id=1, source_target_pairs={{0,2},{1,3},{2,0},{3,1},{4,6},{5,7},{6,4},{7,5},{8,10},{9,11},{10,... | collective-permute-start | bytes 1572872 | tf_op jit(solution)/shard_map/ppermute | solution.py:122
  83.0 21.2 %collective-permute-start.16 = (bf16[128,3456]{1,0:T(8,128)(2,1)S(1)}, bf16[128,3456]{1,0:T(8,128)(2,1)S(1)}, u32[]{:S(2)}, u32[]{:S(2)}) collective-permute-start(bf16[128,3456]{1,0:T(8,128)(2,1)S(1)} %collective-permute-done.12.refs_7_), channel_id=1, source_target_pairs={{0,8},{8,16},{16,24},{24,28},{28,20},{20,12},{12,4},{4,0},{1,9},{9... | collective-permute-start | bytes 2654216 | tf_op jit(solution)/shard_map/ppermute | solution.py:65
  84.6 20.9 %collective-permute-start.17 = (bf16[128,3456]{1,0:T(8,128)(2,1)S(1)}, bf16[128,3456]{1,0:T(8,128)(2,1)S(1)}, u32[]{:S(2)}, u32[]{:S(2)}) collective-permute-start(bf16[128,3456]{1,0:T(8,128)(2,1)S(1)} %collective-permute-done.13.refs_2_), channel_id=1, source_target_pairs={{8,0},{16,8},{24,16},{28,24},{20,28},{12,20},{4,12},{0,4},{9,1},{1... | collective-permute-start | bytes 2654216 | tf_op jit(solution)/shard_map/ppermute | solution.py:65
  86.6 13.3 %collective-permute-start.15 = (bf16[256,1024]{1,0:T(8,128)(2,1)S(1)}, bf16[256,1024]{1,0:T(8,128)(2,1)}, u32[]{:S(2)}, u32[]{:S(2)}) collective-permute-start(bf16[256,1024]{1,0:T(8,128)(2,1)S(1)} %get-tuple-element.108.mine), channel_id=1, source_target_pairs={{0,2},{1,3},{2,0},{3,1},{4,6},{5,7},{6,4},{7,5},{8,10},{9,11},{10,... | collective-permute-start | bytes 1572872 | tf_op jit(solution)/shard_map/ppermute | solution.py:122
  88.1 24.6 %collective-permute-start.14 = (bf16[256,1024]{1,0:T(8,128)(2,1)S(1)}, bf16[256,1024]{1,0:T(8,128)(2,1)}, u32[]{:S(2)}, u32[]{:S(2)}) collective-permute-start(bf16[256,1024]{1,0:T(8,128)(2,1)S(1)} %get-tuple-element.108.mine), channel_id=1, source_target_pairs={{0,1},{1,0},{2,3},{3,2},{4,5},{5,4},{6,7},{7,6},{8,9},{9,8},{10,11... | collective-permute-start | bytes 1572872 | tf_op jit(solution)/shard_map/ppermute | solution.py:122
  105.5 14.3 %collective-permute-start.18 = (bf16[256,1024]{1,0:T(8,128)(2,1)}, bf16[256,1024]{1,0:T(8,128)(2,1)}, u32[]{:S(2)}, u32[]{:S(2)}) collective-permute-start(bf16[256,1024]{1,0:T(8,128)(2,1)} %collective-permute-done.15.far), channel_id=1, source_target_pairs={{0,1},{1,0},{2,3},{3,2},{4,5},{5,4},{6,7},{7,6},{8,9},{9,8},{10,11... | collective-permute-start | bytes 1572872 | tf_op jit(solution)/shard_map/ppermute | solution.py:122
  105.6 12.7 %collective-permute-start.19 = (bf16[64,3456]{1,0:T(8,128)(2,1)S(1)}, bf16[64,3456]{1,0:T(8,128)(2,1)}, u32[]{:S(2)}, u32[]{:S(2)}) collective-permute-start(bf16[64,3456]{1,0:T(8,128)(2,1)S(1)} %slice.165), channel_id=1, source_target_pairs={{0,8},{8,16},{16,24},{24,28},{28,20},{20,12},{12,4},{4,0},{1,9},{9... | collective-permute-start | bytes 1327112 | tf_op jit(solution)/shard_map/ppermute | solution.py:65
  107.2 12.6 %collective-permute-start.20 = (bf16[64,3456]{1,0:T(8,128)(2,1)S(1)}, bf16[64,3456]{1,0:T(8,128)(2,1)}, u32[]{:S(2)}, u32[]{:S(2)}) collective-permute-start(bf16[64,3456]{1,0:T(8,128)(2,1)S(1)} %slice.166), channel_id=1, source_target_pairs={{8,0},{16,8},{24,16},{28,24},{20,28},{12,20},{4,12},{0,4},{9,1},{1... | collective-permute-start | bytes 1327112 | tf_op jit(solution)/shard_map/ppermute | solution.py:65
  148.6 17.0 %collective-permute-start.22 = (bf16[256,1024]{1,0:T(8,128)(2,1)S(1)}, bf16[256,1024]{1,0:T(8,128)(2,1)S(1)}, u32[]{:S(2)}, u32[]{:S(2)}) collective-permute-start(bf16[256,1024]{1,0:T(8,128)(2,1)S(1)} %add_convert_fusion.6), channel_id=1, source_target_pairs={{0,2},{1,3},{2,0},{3,1},{4,6},{5,7},{6,4},{7,5},{8,10},{9,11},{10,... | collective-permute-start | bytes 1572872 | tf_op jit(solution)/shard_map/ppermute | solution.py:122
  157.2 12.0 %collective-permute-start.26 = (bf16[64,3456]{1,0:T(8,128)(2,1)S(1)}, bf16[64,3456]{1,0:T(8,128)(2,1)S(1)}, u32[]{:S(2)}, u32[]{:S(2)}) collective-permute-start(bf16[64,3456]{1,0:T(8,128)(2,1)S(1)} %get-tuple-element.120), channel_id=1, source_target_pairs={{0,8},{8,16},{16,24},{24,28},{28,20},{20,12},{12,4},{4,0},{1,9},{9... | collective-permute-start | bytes 1327112 | tf_op jit(solution)/shard_map/ppermute | solution.py:92
  158.7 11.6 %collective-permute-start.27 = (bf16[64,3456]{1,0:T(8,128)(2,1)S(1)}, bf16[64,3456]{1,0:T(8,128)(2,1)S(1)}, u32[]{:S(2)}, u32[]{:S(2)}) collective-permute-start(bf16[64,3456]{1,0:T(8,128)(2,1)S(1)} %get-tuple-element.121), channel_id=1, source_target_pairs={{8,0},{16,8},{24,16},{28,24},{20,28},{12,20},{4,12},{0,4},{9,1},{1... | collective-permute-start | bytes 1327112 | tf_op jit(solution)/shard_map/ppermute | solution.py:92
  167.4 14.5 %collective-permute-start.24 = (bf16[256,1024]{1,0:T(8,128)(2,1)S(1)}, bf16[256,1024]{1,0:T(8,128)(2,1)S(1)}, u32[]{:S(2)}, u32[]{:S(2)}) collective-permute-start(bf16[256,1024]{1,0:T(8,128)(2,1)S(1)} %get-tuple-element.129.mine), channel_id=1, source_target_pairs={{0,2},{1,3},{2,0},{3,1},{4,6},{5,7},{6,4},{7,5},{8,10},{9,11},{10,... | collective-permute-start | bytes 1572872 | tf_op jit(solution)/shard_map/ppermute | solution.py:122
  167.9 26.8 %collective-permute-start.23 = (bf16[256,1024]{1,0:T(8,128)(2,1)S(1)}, bf16[256,1024]{1,0:T(8,128)(2,1)S(1)}, u32[]{:S(2)}, u32[]{:S(2)}) collective-permute-start(bf16[256,1024]{1,0:T(8,128)(2,1)S(1)} %get-tuple-element.129.mine), channel_id=1, source_target_pairs={{0,1},{1,0},{2,3},{3,2},{4,5},{5,4},{6,7},{7,6},{8,9},{9,8},{10,11... | collective-permute-start | bytes 1572872 | tf_op jit(solution)/shard_map/ppermute | solution.py:122
  170.6 20.3 %collective-permute-start.28 = (bf16[128,3456]{1,0:T(8,128)(2,1)S(1)}, bf16[128,3456]{1,0:T(8,128)(2,1)S(1)}, u32[]{:S(2)}, u32[]{:S(2)}) collective-permute-start(bf16[128,3456]{1,0:T(8,128)(2,1)S(1)} %pad_maximum_fusion), channel_id=1, source_target_pairs={{0,8},{8,16},{16,24},{24,28},{28,20},{20,12},{12,4},{4,0},{1,9},{9... | collective-permute-start | bytes 2654216 | tf_op jit(solution)/shard_map/ppermute | solution.py:92
  171.7 20.4 %collective-permute-start.29 = (bf16[128,3456]{1,0:T(8,128)(2,1)S(1)}, bf16[128,3456]{1,0:T(8,128)(2,1)S(1)}, u32[]{:S(2)}, u32[]{:S(2)}) collective-permute-start(bf16[128,3456]{1,0:T(8,128)(2,1)S(1)} %pad_maximum_fusion.1), channel_id=1, source_target_pairs={{8,0},{16,8},{24,16},{28,24},{20,28},{12,20},{4,12},{0,4},{9,1},{1... | collective-permute-start | bytes 2654216 | tf_op jit(solution)/shard_map/ppermute | solution.py:92
  181.8 12.9 %collective-permute-start.25 = (bf16[256,1024]{1,0:T(8,128)(2,1)S(1)}, bf16[256,1024]{1,0:T(8,128)(2,1)S(1)}, u32[]{:S(2)}, u32[]{:S(2)}) collective-permute-start(bf16[256,1024]{1,0:T(8,128)(2,1)S(1)} %collective-permute-done.24.far), channel_id=1, source_target_pairs={{0,1},{1,0},{2,3},{3,2},{4,5},{5,4},{6,7},{7,6},{8,9},{9,8},{10,11... | collective-permute-start | bytes 1572872 | tf_op jit(solution)/shard_map/ppermute | solution.py:122
  191.1 20.4 %collective-permute-start.32 = (bf16[128,3456]{1,0:T(8,128)(2,1)S(1)}, bf16[128,3456]{1,0:T(8,128)(2,1)}, u32[]{:S(2)}, u32[]{:S(2)}) collective-permute-start(bf16[128,3456]{1,0:T(8,128)(2,1)S(1)} %add_convert_fusion.3), channel_id=1, source_target_pairs={{0,8},{8,16},{16,24},{24,28},{28,20},{20,12},{12,4},{4,0},{1,9},{9... | collective-permute-start | bytes 2654216 | tf_op jit(solution)/shard_map/ppermute | solution.py:92
  193.5 19.2 %collective-permute-start.33 = (bf16[128,3456]{1,0:T(8,128)(2,1)S(1)}, bf16[128,3456]{1,0:T(8,128)(2,1)}, u32[]{:S(2)}, u32[]{:S(2)}) collective-permute-start(bf16[128,3456]{1,0:T(8,128)(2,1)S(1)} %add_convert_fusion.2), channel_id=1, source_target_pairs={{8,0},{16,8},{24,16},{28,24},{20,28},{12,20},{4,12},{0,4},{9,1},{1... | collective-permute-start | bytes 2654216 | tf_op jit(solution)/shard_map/ppermute | solution.py:92
  214.7 23.1 %collective-permute-start.39 = (bf16[128,3456]{1,0:T(8,128)(2,1)S(1)}, bf16[128,3456]{1,0:T(8,128)(2,1)S(1)}, u32[]{:S(2)}, u32[]{:S(2)}) collective-permute-start(bf16[128,3456]{1,0:T(8,128)(2,1)S(1)} %get-tuple-element.163), channel_id=1, source_target_pairs={{8,0},{16,8},{24,16},{28,24},{20,28},{12,20},{4,12},{0,4},{9,1},{1... | collective-permute-start | bytes 2654216 | tf_op jit(solution)/shard_map/ppermute | solution.py:92
  215.8 22.0 %collective-permute-start.38 = (bf16[128,3456]{1,0:T(8,128)(2,1)S(1)}, bf16[128,3456]{1,0:T(8,128)(2,1)S(1)}, u32[]{:S(2)}, u32[]{:S(2)}) collective-permute-start(bf16[128,3456]{1,0:T(8,128)(2,1)S(1)} %get-tuple-element.164), channel_id=1, source_target_pairs={{0,8},{8,16},{16,24},{24,28},{28,20},{20,12},{12,4},{4,0},{1,9},{9... | collective-permute-start | bytes 2654216 | tf_op jit(solution)/shard_map/ppermute | solution.py:92
  228.8 26.2 %collective-permute-start.30 = (bf16[512,1024]{1,0:T(8,128)(2,1)S(1)}, bf16[512,1024]{1,0:T(8,128)(2,1)S(1)}, u32[]{:S(2)}, u32[]{:S(2)}) collective-permute-start(bf16[512,1024]{1,0:T(8,128)(2,1)S(1)} %copy-done.40), channel_id=1, source_target_pairs={{0,1},{1,0},{2,3},{3,2},{4,5},{5,4},{6,7},{7,6},{8,9},{9,8},{10,11... | collective-permute-start | bytes 3145736 | tf_op jit(solution)/shard_map/ppermute | solution.py:122
  235.7 11.7 %collective-permute-start.34 = (bf16[512,1024]{1,0:T(8,128)(2,1)S(1)}, bf16[512,1024]{1,0:T(8,128)(2,1)S(1)}, u32[]{:S(2)}, u32[]{:S(2)}) collective-permute-start(bf16[512,1024]{1,0:T(8,128)(2,1)S(1)} %get-tuple-element.146), channel_id=1, source_target_pairs={{0,1},{1,0},{2,3},{3,2},{4,5},{5,4},{6,7},{7,6},{8,9},{9,8},{10,11... | collective-permute-start | bytes 3145736 | tf_op jit(solution)/shard_map/ppermute | solution.py:122
  238.5 12.0 %collective-permute-start.40 = (bf16[144,768]{1,0:T(8,128)(2,1)S(1)}, bf16[144,768]{1,0:T(8,128)(2,1)S(1)}, u32[]{:S(2)}, u32[]{:S(2)}) collective-permute-start(bf16[144,768]{1,0:T(8,128)(2,1)S(1)} %pad_maximum_fusion.2), channel_id=1, source_target_pairs={{0,8},{8,16},{16,24},{24,28},{28,20},{20,12},{12,4},{4,0},{1,9},{9... | collective-permute-start | bytes 663560 | tf_op jit(solution)/shard_map/ppermute | solution.py:92
  247.5 15.8 %collective-permute-start.35 = (bf16[256,1024]{1,0:T(8,128)(2,1)S(1)}, bf16[256,1024]{1,0:T(8,128)(2,1)S(1)}, u32[]{:S(2)}, u32[]{:S(2)}) collective-permute-start(bf16[256,1024]{1,0:T(8,128)(2,1)S(1)} %add_convert_fusion.4), channel_id=1, source_target_pairs={{0,2},{1,3},{2,0},{3,1},{4,6},{5,7},{6,4},{7,5},{8,10},{9,11},{10,... | collective-permute-start | bytes 1572872 | tf_op jit(solution)/shard_map/ppermute | solution.py:122
  255.2 18.9 %collective-permute-start.31 = (bf16[256,1024]{1,0:T(8,128)(2,1)S(1)}, bf16[256,1024]{1,0:T(8,128)(2,1)S(1)}, u32[]{:S(2)}, u32[]{:S(2)}) collective-permute-start(bf16[256,1024]{1,0:T(8,128)(2,1)S(1)} %add_convert_fusion.5), channel_id=1, source_target_pairs={{0,2},{1,3},{2,0},{3,1},{4,6},{5,7},{6,4},{7,5},{8,10},{9,11},{10,... | collective-permute-start | bytes 1572872 | tf_op jit(solution)/shard_map/ppermute | solution.py:122
  271.8 8.2 %collective-permute-start.48 = (f32[8,384]{1,0:T(8,128)S(1)}, f32[8,384]{1,0:T(8,128)S(1)}, u32[]{:S(2)}, u32[]{:S(2)}) collective-permute-start(f32[8,384]{1,0:T(8,128)S(1)} %get-tuple-element.155), channel_id=1, source_target_pairs={{0,3},{1,2},{2,1},{3,0},{4,7},{5,6},{6,5},{7,4},{8,11},{9,10},{10,... | collective-permute-start | bytes 36872 | tf_op jit(solution)/shard_map/ppermute | solution.py:122
  271.8 8.2 %collective-permute-start.47 = (f32[8,384]{1,0:T(8,128)S(1)}, f32[8,384]{1,0:T(8,128)S(1)}, u32[]{:S(2)}, u32[]{:S(2)}) collective-permute-start(f32[8,384]{1,0:T(8,128)S(1)} %get-tuple-element.155), channel_id=1, source_target_pairs={{0,2},{1,3},{2,0},{3,1},{4,6},{5,7},{6,4},{7,5},{8,10},{9,11},{10,... | collective-permute-start | bytes 36872 | tf_op jit(solution)/shard_map/ppermute | solution.py:122
  (64 other events, 519.4 us)
where the time goes:
time: 282 us; the launch traced here: 281 us
  Pallas kernels  110 us (39%)
  waiting for transfers between devices  94.8 us (34%)
  starting transfers between devices  48.3 us (17%)
  local copies, waits for them, and re-layouts  14.4 us (5%)
  other arithmetic  12.1 us (4%)
    ppermute x8, waiting for transfers between devices, send(): lax.ppermute(up, 'dp', ahead)  38.2 us
    pallas_call x1, Pallas kernels, feed_forward(): pl.pallas_call(ffn_kernel, grid=(2,), out_shape=(shape_of(slots, width),...  24.5 us
    pallas_call x3, Pallas kernels, feed_forward_weights(): pl.pallas_call(ffn_weights_kernel, grid=(number,), out_shape=(shape_of(nu...  20.6 us
    ppermute x8, waiting for transfers between devices, send(): lax.ppermute(self.moving[0], 'dp', ahead)  19.3 us
    ppermute x17, waiting for transfers between devices, swap(): return lax.ppermute(values, axis, [(i, i ^ bit) for i in range(count)])  18.3 us
    pallas_call x1, Pallas kernels, per_device(): pl.pallas_call(backward_kernel, out_shape=(shape_of(slots, 2 * LANES, dty...  16.7 us
    ppermute x17, starting transfers between devices, swap(): return lax.ppermute(values, axis, [(i, i ^ bit) for i in range(count)])  14.3 us
    ppermute x8, waiting for transfers between devices, send(): lax.ppermute(self.moving[1], 'dp', back)  13.3 us
  transfers between devices with their start and end apart: 49, of which 25 were waited for; matrix products, arithmetic and copies ran while one was open for 4% of the time, Pallas kernels for 30%

commit v1 on v0

--- a/solution.py
+++ b/solution.py
@@ -96,8 +96,8 @@
         up, down = self.moving
         mine_up, mine_down = self.blocks(self.step), self.blocks(self.count - self.step)
         if self.step == self.count // 2 - 1:
-            up = jnp.concatenate([add(mine_up[:HD], up), mine_up[HD:]], axis=0)
-            down = jnp.concatenate([mine_down[:HD], add(mine_down[HD:], down)], axis=0)
+            up = add(mine_up, jnp.pad(up, ((0, mine_up.shape[0] - HD), (0, 0))))
+            down = add(mine_down, jnp.pad(down, ((HD, 0), (0, 0))))
         else:
             up, down = add(mine_up, up), add(mine_down, down)
         self.moving = (up, down)
@@ -492,11 +492,13 @@
         out[:, k * LANES : (k + 1) * LANES] = tokens[:, pl.ds(column(place, k, ring), LANES)]
 
 
-def arrange_live_kernel(ring, place, cotangent, places, out):
+def arrange_live_kernel(ring, place, cotangent, places, out, turned):
     live = places[...] >= 0
     for k in range(cotangent.shape[1] // LANES):
         values = cotangent[:, pl.ds(column(place, k, ring), LANES)].astype(f32)
-        out[:, k * LANES : (k + 1) * LANES] = jnp.where(live, values, 0.0).astype(bf16)
+        values = jnp.where(live, values, 0.0)
+        out[:, k * LANES : (k + 1) * LANES] = values.astype(bf16)
+        turned[k * LANES : (k + 1) * LANES, :] = values.T.astype(bf16)
 
 
 def residual_kernel(part, other, far, tokens, gains, residual, low):
@@ -538,9 +540,9 @@
     put_columns(ring, place, out, grad[...] + norm_back(upstream, gains[0:1, :], normed, inverse))
 
 
-def ffn_kernel(near, near_far, mine, far, output_low, *refs):
+def ffn_kernel(near, near_far, mine, far, output_low, output_t, *refs):
     pieces, rest = refs[:9], refs[9:]
-    low, active, out_send, out_keep, in_send, in_keep, weights = rest
+    low_t, active, out_send, out_keep, in_send, in_keep, first_grad, top, bottom, weights, low, low_pair = rest
     size = mine.shape[0]
     step = weights.shape[1] // 3
     half = pl.program_id(0)
@@ -556,32 +558,43 @@
         low[:size, :] = mine[...]
         low[size:, :] = far[...]
 
-    both = product(low[...], weights[:, : 2 * step])
-    hidden_grad = product(output_low[...], weights[:, 2 * step :])
-    gate, up = both[:, :step], both[:, step:]
-    sigmoid = 1.0 / (1.0 + jnp.exp(-gate))
-    silu = gate * sigmoid
-    active[:, 2 * step :] = (silu * up).astype(bf16)
-    active[:, :step] = (hidden_grad * up * (sigmoid + silu * (1.0 - sigmoid))).astype(bf16)
-    active[:, step : 2 * step] = (hidden_grad * silu).astype(bf16)
-    out = contract_cols(active[:, 2 * step :], weights[:, 2 * step :])
-    into = contract_cols(active[:, : 2 * step], weights[:, : 2 * step])
+    low_t[...] = low[...].T
+    here = pl.ds(pl.multiple_of(half * 2 * size, 2 * size), 2 * size)
+    pair = slice(weights.shape[0] // 2, weights.shape[0] // 2 + 2 * LANES)
+    for first in range(0, step, 256):
+        last = min(first + 256, step)
+        gate = product(low[...], weights[:, first:last])
+        up = product(low[...], weights[:, step + first : step + last])
+        hidden_grad = product(output_low[...], weights[:, 2 * step + first : 2 * step + last])
+        sigmoid = 0.5 + 0.5 * jnp.tanh(0.5 * gate)
+        silu = gate * sigmoid
+        active[here, 2 * step + first : 2 * step + last] = (silu * up).astype(bf16)
+        active[here, first:last] = (hidden_grad * up * (sigmoid + silu * (1.0 - sigmoid))).astype(bf16)
+        active[here, step + first : step + last] = (hidden_grad * silu).astype(bf16)
+    out = contract_cols(active[here, 2 * step :], weights[:, 2 * step :])
+    into = contract_cols(active[here, : 2 * step], weights[:, : 2 * step])
 
     @pl.when(half == 0)
     def _():
         out_send[...] = out.astype(bf16)
         in_send[...] = into.astype(bf16)
+        low_pair[:, : 2 * size] = low_t[pair, :]
 
     @pl.when(half == 1)
     def _():
         out_keep[...] = out.astype(bf16)
         in_keep[...] = into.astype(bf16)
-
-
-def ffn_weights_kernel(low, output_low, active, out, top, bottom):
+        low_pair[:, 2 * size :] = low_t[pair, :]
+        first_grad[:, : 2 * step] = product(low_pair[...], active[:, : 2 * step]).astype(bf16)
+        first_grad[:, 2 * step :] = product(output_t[...], active[:, 2 * step :]).astype(bf16)
+        top[...] = first_grad[:HD, :]
+        bottom[...] = first_grad[HD:LANES, :]
+
+
+def ffn_weights_kernel(low_t, output_t, active, out, top, bottom):
     step = active.shape[1] // 3
-    out[:, : 2 * step] = product(low[...].T, active[:, : 2 * step]).astype(bf16)
-    out[:, 2 * step :] = product(output_low[...].T, active[:, 2 * step :]).astype(bf16)
+    out[:, : 2 * step] = product(low_t[...], active[:, : 2 * step]).astype(bf16)
+    out[:, 2 * step :] = product(output_t[...], active[:, 2 * step :]).astype(bf16)
 
     @pl.when(pl.program_id(0) == 0)
     def _():
@@ -597,8 +610,8 @@
     return pltpu.CompilerParams(vmem_limit_bytes=mebibytes * 2**20)
 
 
-def cost(flops, bytes_moved, exps=0):
-    return pl.CostEstimate(flops=int(flops), bytes_accessed=int(bytes_moved), transcendentals=int(exps))
+def cost(flops, bytes_moved, exps=0, share=1.0):
+    return pl.CostEstimate(flops=int(share * flops), bytes_accessed=int(share * bytes_moved), transcendentals=int(share * exps))
 
 
 def simple(kernel, outs, name, args, n_scalars=0):
@@ -631,7 +644,7 @@
     )(*([place] if place is not None else []), *args)
 
 
-def feed_forward(rows_in, output_low, pieces):
+def feed_forward(rows_in, output_low, output_t, pieces):
     slots, width = output_low.shape
     cols = pieces[0].shape[1]
     half = slots // 2
@@ -640,22 +653,25 @@
     return pl.pallas_call(
         ffn_kernel,
         grid=(2,),
-        out_shape=(shape_of(slots, width), shape_of(slots, cols), wide, wide, wide, wide),
-        in_specs=[whole_vmem] * 4 + [moving(width)] + [whole_vmem] * 9,
-        out_specs=(moving(width), moving(cols)) + (whole_vmem,) * 4,
-        scratch_shapes=[pltpu.VMEM((width, cols), bf16)],
+        out_shape=(shape_of(width, slots), shape_of(slots, cols), wide, wide, wide, wide)
+        + (shape_of(2 * LANES, cols), shape_of(HD, cols), shape_of(HD, cols)),
+        in_specs=[whole_vmem] * 4
+        + [moving(width), pl.BlockSpec((2 * LANES, slots), lambda i: (width // (4 * LANES), 0))]
+        + [whole_vmem] * 9,
+        out_specs=(pl.BlockSpec((width, half), lambda i: (0, i)), whole_vmem) + (whole_vmem,) * 7,
+        scratch_shapes=[pltpu.VMEM((width, cols), bf16), pltpu.VMEM((half, width), bf16), pltpu.VMEM((2 * LANES, slots), bf16)],
         compiler_params=params(56),
         cost_estimate=cost(4 * slots * width * cols, 20 * 2**20, 2e6),
         name="ffn",
-    )(*rows_in, output_low, *pieces)
-
-
-def feed_forward_weights(low, output_low, active, first, number):
-    slots, width = low.shape
+    )(*rows_in, output_low, output_t, *pieces)
+
+
+def feed_forward_weights(low_t, output_t, active, first, number):
+    width, slots = low_t.shape
     cols = active.shape[1]
     pair = 2 * LANES
     pairs = width // pair
-    side = pl.BlockSpec((slots, pair), lambda i: (0, lax.rem(i + first, pairs)))
+    side = pl.BlockSpec((pair, slots), lambda i: (lax.rem(i + first, pairs), 0))
     return pl.pallas_call(
         ffn_weights_kernel,
         grid=(number,),
@@ -665,7 +681,7 @@
         compiler_params=params(),
         cost_estimate=cost(2 * slots * pair * number * cols, 12 * 2**20),
         name="ffn_weights",
-    )(low, output_low, active)
+    )(low_t, output_t, active)
 
 
 def rotary_tables(slot_positions):
@@ -703,9 +719,15 @@
         gains_row = jnp.pad(
             jnp.concatenate([attn_gain, ffn_gain])[None, :], ((0, 15), (0, attn_cols - 2 * LANES))
         )
-        attn_block = simple(
-            pack_kernel, shape_of(LANES + 16, attn_cols), "pack", (w_query, w_key, w_value, w_out, gains_row)
-        )
+        shards = (w_query, w_key, w_value, w_out, gains_row)
+        attn_block = pl.pallas_call(
+            pack_kernel,
+            grid=(1,),
+            out_shape=shape_of(LANES + 16, attn_cols),
+            in_specs=[first_rows(*a.shape) for a in shards],
+            out_specs=first_rows(LANES + 16, attn_cols),
+            name="pack",
+        )(*shards)
         ffn_block = simple(pack_ffn_kernel, shape_of(LANES, 3 * hidden), "pack_ffn", (w_gate, w_up, w_down))
     else:
         gathered = lax.all_gather(
@@ -722,34 +744,36 @@
             )
             attn_pieces.append(piece if k == 4 else jnp.concatenate([piece, pad], axis=0))
         turned = w_down.T
-        block = jnp.concatenate([w_gate, w_up, turned], axis=1)
-        ffn_pieces = pieces_of(lax.all_gather(block, "dp", axis=0, tiled=True))
+        block = lax.all_gather(jnp.concatenate([w_gate, w_up, turned], axis=1), "dp", axis=0, tiled=True)
+        ffn_pieces = pieces_of(block)
 
     places = jnp.broadcast_to(positions[:, None], (slots, LANES))
     place_rows = positions.reshape(4, 1, rows)
     straight = pl.BlockSpec((rows, width), lambda i, s: (i, 0))
 
-    def arranged(kernel, row_of, args, name):
+    def arranged(kernel, row_of, args, name, turned=False):
         return pl.pallas_call(
             in_place(kernel),
-            out_shape=shape_of(slots, width),
+            out_shape=(shape_of(slots, width), shape_of(width, slots)) if turned else shape_of(slots, width),
             grid_spec=pltpu.PrefetchScalarGridSpec(
                 num_scalar_prefetch=1,
                 grid=(4,),
                 in_specs=[pl.BlockSpec((rows, a.shape[1]), lambda i, s: (row_of(i) ^ s[0], 0)) for a in args],
-                out_specs=straight,
+                out_specs=(straight, pl.BlockSpec((width, rows), lambda i, s: (0, i))) if turned else straight,
             ),
             cost_estimate=cost(0, 4 * slots * width),
             name=name,
         )(place, *args)
 
     inputs = arranged(arrange_kernel, lambda i: i, (tokens,), "arrange")
-    output_low = arranged(arrange_live_kernel, lambda i: lax.rem(2 * i + 1, 5), (cotangent, places), "arrange_live")
+    output_low, output_t = arranged(
+        arrange_live_kernel, lambda i: lax.rem(2 * i + 1, 5), (cotangent, places), "arrange_live", True
+    )
     tables = rotary_tables(positions)
     if ring:
         attn_ring, ffn_ring = RingGather(attn_block, count), RingGather(ffn_block, count)
         attn_ring.send()
-        attn_ring.tie(*ffn_ring.moving)
+        attn_ring.tie(ffn_block)
         attn_ring.send()
         (inputs,) = attn_ring.tie(inputs)
         attn_ring.send()
@@ -811,19 +835,19 @@
     )
     near, far = swap(ffn_rows, "tensor", 1), swap(ffn_rows, "tensor", 2)
     if ring:
-        (far,) = after((far,), ffn_ring.moving)
         ffn_ring.send()
         ffn_pieces = ffn_ring.pieces()
     rows_in = near, swap(far, "tensor", 1), ffn_rows, far
 
-    ffn_low, active, out_send, out_keep, in_send, in_keep = feed_forward(rows_in, output_low, ffn_pieces)
+    ffn_low_t, active, out_send, out_keep, in_send, in_keep, first_grad, top, bottom = feed_forward(
+        rows_in, output_low, output_t, ffn_pieces
+    )
     other = swap(in_send, "tensor", 1)
     if ring:
         half = count // 2
         toward_y = add(in_keep[rows:], other[rows:])
         (active,) = after((active,), (toward_y,))
-        first_grad, top, bottom = feed_forward_weights(ffn_low, output_low, active, half // 2, 1)
-        next_grad, _, _ = feed_forward_weights(ffn_low, output_low, active, half // 2 - 1, 1)
+        next_grad, _, _ = feed_forward_weights(ffn_low_t, output_t, active, half // 2 - 1, 1)
         ffn_grads = {half // 2: first_grad, half // 2 - 1: next_grad}
 
         def ffn_block_of(k):
@@ -833,22 +857,28 @@
         ffn_scatter.send()
         far = swap(toward_y, "tensor", 2)
     else:
-        grad_ffn, _, _ = feed_forward_weights(ffn_low, output_low, active, 0, width // (2 * LANES))
+        grad_ffn, _, _ = feed_forward_weights(ffn_low_t, output_t, active, 0, width // (2 * LANES))
         far = swap(add(in_keep[rows:], other[rows:]), "tensor", 2)
     residual_grad, residual_low, ffn_gain_part = own_rows(
         residual_back_kernel, rows, width, (row_f32, row_bf16, one_gain), "residual_back", None,
         (in_keep, other, far, residual, gains, output_low), [(5, 2)],
     )
-    rows_back = tensor_gather(residual_low)
+    near, far = swap(residual_low, "tensor", 1), swap(residual_low, "tensor", 2)
+    out_other = swap(out_send, "tensor", 1)
+    out_toward_y = add(out_keep[rows:], out_other[rows:])
+    if ring:
+        (far,), (out_toward_y,) = tied((far,), (out_toward_y,))
+    out_far = swap(out_toward_y, "tensor", 2)
+    rows_back = near, swap(far, "tensor", 1), residual_low, far
     if ring:
         (active,) = after((active,), (residual_low,))
         ffn_scatter.moving = after(ffn_scatter.moving, (residual_low,))
         ffn_scatter.add()
         ffn_scatter.send()
-        rest_grad, _, _ = feed_forward_weights(ffn_low, output_low, active, half // 2 + 1, half // 2)
+        rest_grad, _, _ = feed_forward_weights(ffn_low_t, output_t, active, half // 2 + 1, half // 2)
         ffn_grads[half // 2 + 1], ffn_grads[0] = rest_grad[: 2 * LANES], rest_grad[2 * LANES :]
         ffn_scatter.add()
-        rows_back = after(rows_back, ffn_scatter.moving)
+        rows_back = after(rows_back, (*ffn_scatter.moving, out_far))
         ffn_scatter.send()
 
     grads = pl.pallas_call(
@@ -900,8 +930,6 @@
         ffn_gain_part, *grads,
     )
 
-    (out_send,) = after((out_send,), rows_back)
-    out_other, out_far = tensor_scatter(out_send, out_keep)
     (block_output,) = own_rows(
         in_place(output_kernel), rows, width, (row_bf16,), "output", place, (out_keep, out_other, out_far, residual)
     )
@@ -913,12 +941,18 @@
     if ring:
         attn_scatter = RingScatter(lambda k: grad_attn[k * tall : (k + 1) * tall], top, bottom, count)
         attn_scatter.send()
+        shard_gate, shard_up, shard_down = simple(
+            unpack_ffn_kernel,
+            tuple(jax.ShapeDtypeStruct(w.shape, f32) for w in (w_gate, w_up, w_down)),
+            "unpack_ffn",
+            (ffn_block_of(0), *ffn_scatter.moving),
+        )
         for step in range(half - 1):
             attn_scatter.add()
             if step == 0:
                 attn_scatter.moving = after(attn_scatter.moving, ffn_scatter.moving)
             if step == half - 2:
-                attn_scatter.moving = after(attn_scatter.moving, (far,))
+                attn_scatter.moving = after(attn_scatter.moving, (far, shard_gate, block_output))
             attn_scatter.send()
         shard_query, shard_key, shard_value, shard_out, gain_part = simple(
             unpack_kernel,
@@ -929,12 +963,6 @@
         gain_total = gain_part + sum(swap(gain_part, "tensor", bits) for bits in (1, 2, 3))
         grad_attn_gain, grad_ffn_gain, heads = (gain_total[0, k * LANES : (k + 1) * LANES] for k in range(3))
         grad_query_gain, grad_key_gain = heads[:HD], heads[HD:]
-        shard_gate, shard_up, shard_down = simple(
-            unpack_ffn_kernel,
-            tuple(jax.ShapeDtypeStruct(w.shape, f32) for w in (w_gate, w_up, w_down)),
-            "unpack_ffn",
-            (ffn_block_of(0), *ffn_scatter.moving),
-        )
     else:
         gain_total = sum_all(jnp.concatenate([attn_gain_part, ffn_gain_part, head_gains[0:1]], axis=1))[0]
         share = width // count

time: 282 us -> 275 us (0.975)
  local copies, waits for them, and re-layouts: 14.4 us -> 9.67 us
  other arithmetic: 12.1 us -> 15.2 us
  starting transfers between devices: 48.3 us -> 45.2 us
    pallas_call x3 -> x4, Pallas kernels: 34.1 us -> 40.5 us  [the longest x1 28.8 us: feed_forward(): pl.pallas_call(ffn_kernel, grid=(2,), out_shape=(shape_of(width, slots),...]
    pallas_call x3 -> x2, Pallas kernels: 20.6 us -> 14.9 us  [feed_forward_weights(): pl.pallas_call(ffn_weights_kernel, grid=(number,), out_shape=(shape_of(nu...]
    unnamed x94 -> x80, local copies, waits for them, and re-layouts: 9.6 us -> 4.98 us
    ppermute x17, starting transfers between devices: 14.3 us -> 11 us  [swap(): return lax.ppermute(values, axis, [(i, i ^ bit) for i in range(count)])]
    convert_element_type x14 -> x13, other arithmetic: 8.75 us -> 12 us  [add(): return (left.astype(f32) + right.astype(f32)).astype(bf16)]
  transfers between devices with their start and end apart: 49 -> 49, of which waited for: 25 -> 25; matrix products, arithmetic and copies ran while one was open for 4% -> 5% of each run, Pallas kernels for 30% -> 29%
where the time goes in v1:
time: 275 us; the launch traced here: 274 us
  Pallas kernels  111 us (40%)
  waiting for transfers between devices  92.6 us (34%)
  starting transfers between devices  45.2 us (16%)
  other arithmetic  15.2 us (6%)
  local copies, waits for them, and re-layouts  9.67 us (4%)
    ppermute x8, waiting for transfers between devices, send(): lax.ppermute(up, 'dp', ahead)  36.1 us
    pallas_call x1, Pallas kernels, feed_forward(): pl.pallas_call(ffn_kernel, grid=(2,), out_shape=(shape_of(width, slots),...  28.8 us
    ppermute x8, waiting for transfers between devices, send(): lax.ppermute(self.moving[0], 'dp', ahead)  21.6 us
    ppermute x17, waiting for transfers between devices, swap(): return lax.ppermute(values, axis, [(i, i ^ bit) for i in range(count)])  16.7 us
    pallas_call x1, Pallas kernels, per_device(): pl.pallas_call(backward_kernel, out_shape=(shape_of(slots, 2 * LANES, dty...  16.4 us
    pallas_call x2, Pallas kernels, feed_forward_weights(): pl.pallas_call(ffn_weights_kernel, grid=(number,), out_shape=(shape_of(nu...  14.9 us
    ppermute x8, waiting for transfers between devices, send(): lax.ppermute(self.moving[1], 'dp', back)  13.3 us
    convert_element_type x13, other arithmetic, add(): return (left.astype(f32) + right.astype(f32)).astype(bf16)  12 us
  transfers between devices with their start and end apart: 49, of which 25 were waited for; matrix products, arithmetic and copies ran while one was open for 5% of the time, Pallas kernels for 29%

profile of v1, /device:TPU:0, one launch (start us, length us, event | category | flops | bytes accessed | tf_op | source)
XLA Modules:
  0.0 274.4 jit_solution(9816337042516189996)
XLA Ops:
  1.9 1.7 pack.1.p0
  3.6 2.9 %collective-permute-start.1 = (bf16[144,768]{1,0:T(8,128)(2,1)}, bf16[144,768]{1,0:T(8,128)(2,1)S(1)}, u32[]{:S(2)}, u32[]{:S(2)}) collective-permute-start(bf16[144,768]{1,0:T(8,128)(2,1)} %pack.1.p0), channel_id=1, source_target_pairs={{8,0},{16,8},{24,16},{28,24},{20,28},{12,20},{4,12},{0,4},{9,1},{1... | collective-permute-start | bytes 663560 | tf_op jit(solution)/shard_map/ppermute | solution.py:65
  7.2 4.8 %arrange.1.tokens = bf16[1024,1024]{1,0:T(8,128)(2,1)} custom-call(s32[2]{0:T(128)} %pad_add_fusion.place, bf16[1024,1024]{1,0:T(8,128)(2,1)} %tokens.1), custom_call_target="tpu_custom_call" | custom-call | bytes 4194304 | tf_op jit(solution)/shard_map/arrange/pallas_call | solution.py:755
  15.7 3.9 %collective-permute-done.2.p7 = bf16[144,768]{1,0:T(8,128)(2,1)S(1)} collective-permute-done((bf16[144,768]{1,0:T(8,128)(2,1)S(1)}, bf16[144,768]{1,0:T(8,128)(2,1)S(1)}, u32[]{:S(2)}, u32[]{:S(2)}) %collective-permute-start.2) | collective-permute-done | bytes 221216 | tf_op jit(solution)/shard_map/ppermute | solution.py:65
  22.8 1.9 multiply_sine_fusion
  24.7 2.0 collective-permute-done.4.p6
  31.8 4.2 %collective-permute-done.6.p4 = bf16[64,768]{1,0:T(8,128)(2,1)} collective-permute-done((bf16[64,768]{1,0:T(8,128)(2,1)}, bf16[64,768]{1,0:T(8,128)(2,1)}, u32[]{:S(2)}, u32[]{:S(2)}) %collective-permute-start.6) | collective-permute-done | bytes 98336 | tf_op jit(solution)/shard_map/ppermute | solution.py:65
  38.0 8.3 %project.1 = (bf16[1024,768]{1,0:T(8,128)(2,1)}, f32[8,1024]{1,0:T(8,128)S(1)}, bf16[1024,1024]{1,0:T(8,128)(2,1)}, f32[1024,512]{1,0:T(8,128)}, bf16[1024,256]{...) custom-call(s32[2]{0:T(128)S(1)} %copy-done.14, ...), custom_call_target="tpu_custom_call" | custom-call | flops 3000000000 | bytes 14680064 | tf_op jit(solution)/shard_map/project/pallas_call | solution.py:788
  47.9 10.2 %attention.1 = (bf16[1024,256]{1,0:T(8,128)(2,1)S(1)}, f32[1024,256]{1,0:T(8,128)S(1)}, bf16[512,1024]{1,0:T(8,128)(2,1)S(1)}, bf16[512,1024]{1,0:T(8,128)(2,1)S(1)}) custom-call(s32[2]{0:T(128)S(1)} %copy-done.14, s32[1024,128]{1,0:T(8,128)S(1)} %broadcast_in_dim.4.places, bf16[1024,768]{1,0:T(8,128)(2,1)} %get-tuple-element.99.weights, ...), custom_call_target="tpu_custom_call" | custom-call | flops 8999999488 | bytes 8388608 | tf_op jit(solution)/shard_map/attention/pallas_call | solution.py:808
  63.6 17.6 %collective-permute-done.12.refs_7_ = bf16[128,3456]{1,0:T(8,128)(2,1)S(1)} collective-permute-done((bf16[128,3456]{1,0:T(8,128)(2,1)S(1)}, bf16[128,3456]{1,0:T(8,128)(2,1)S(1)}, u32[]{:S(2)}, u32[]{:S(2)}) %collective-permute-start.12) | collective-permute-done | bytes 884768 | tf_op jit(solution)/shard_map/ppermute | solution.py:65
  86.3 11.7 %collective-permute-done.15.far = bf16[256,1024]{1,0:T(8,128)(2,1)} collective-permute-done((bf16[256,1024]{1,0:T(8,128)(2,1)S(1)}, bf16[256,1024]{1,0:T(8,128)(2,1)}, u32[]{:S(2)}, u32[]{:S(2)}) %collective-permute-start.15) | collective-permute-done | bytes 524320 | tf_op jit(solution)/shard_map/ppermute | solution.py:122
  98.0 4.4 %collective-permute-done.18.refs_6_ = bf16[128,3456]{1,0:T(8,128)(2,1)S(1)} collective-permute-done((bf16[128,3456]{1,0:T(8,128)(2,1)S(1)}, bf16[128,3456]{1,0:T(8,128)(2,1)S(1)}, u32[]{:S(2)}, u32[]{:S(2)}) %collective-permute-start.18) | collective-permute-done | bytes 884768 | tf_op jit(solution)/shard_map/ppermute | solution.py:65
  105.6 5.3 %arrange_live.1 = (bf16[1024,1024]{1,0:T(8,128)(2,1)}, bf16[1024,1024]{1,0:T(8,128)(2,1)}) custom-call(s32[2]{0:T(128)} %pad_add_fusion.place, bf16[1024,1024]{1,0:T(8,128)(2,1)} %cotangent.1, s32[1024,128]{1,0:T(8,128)} %copy-done.4), custom_call_target="tpu_custom_call" | custom-call | bytes 4194304 | tf_op jit(solution)/shard_map/arrange_live/pallas_call | solution.py:755
  110.9 2.6 collective-permute-done.19.refs_4_
  113.4 2.3 collective-permute-done.20.refs_5_
  115.7 28.8 %ffn.1 = (bf16[1024,1024]{1,0:T(8,128)(2,1)}, bf16[1024,3456]{1,0:T(8,128)(2,1)}, bf16[512,1024]{1,0:T(8,128)(2,1)}, bf16[512,1024]{1,0:T(8,128)(2,1)}, bf16[512...) custom-call(bf16[256,1024]{1,0:T(8,128)(2,1)} %collective-permute-do, ...), custom_call_target="tpu_custom_call" | custom-call | flops 14495514624 | bytes 20971520 | tf_op jit(solution)/shard_map/ffn/pallas_call | solution.py:653
  145.1 2.4 collective-permute-done.22.other
  153.8 6.2 %ffn_weights.2 = (bf16[256,3456]{1,0:T(8,128)(2,1)S(1)}, bf16[64,3456]{1,0:T(8,128)(2,1)}, bf16[64,3456]{1,0:T(8,128)(2,1)}) custom-call(bf16[1024,1024]{1,0:T(8,128)(2,1)S(1)} %copy-done.6, bf16[1024,1024]{1,0:T(8,128)(2,1)} %get-tuple-element.112.output_t, bf16[1024,3456]{1,0:T(8,128)(2,1)} %get-tuple-element.133.active), custom_call_target="tpu_custom_call" | custom-call | flops 1811939328 | bytes 12582912 | tf_op jit(solution)/shard_map/ffn_weights/pallas_call | solution.py:675
  161.0 1.6 collective-permute-done.23.far
  162.7 1.7 residual_back.1
  169.7 8.8 %ffn_weights.3 = (bf16[512,3456]{1,0:T(8,128)(2,1)}, bf16[64,3456]{1,0:T(8,128)(2,1)}, bf16[64,3456]{1,0:T(8,128)(2,1)}) custom-call(bf16[1024,1024]{1,0:T(8,128)(2,1)S(1)} %copy-done.7, bf16[1024,1024]{1,0:T(8,128)(2,1)S(1)} %copy-done.5, bf16[1024,3456]{1,0:T(8,128)(2,1)} %get-tuple-element.133.active), custom_call_target="tpu_custom_call" | custom-call | flops 3623878656 | bytes 12582912 | tf_op jit(solution)/shard_map/ffn_weights/pallas_call | solution.py:675
  180.3 7.7 %collective-permute-done.30 = bf16[128,3456]{1,0:T(8,128)(2,1)} collective-permute-done((bf16[128,3456]{1,0:T(8,128)(2,1)S(1)}, bf16[128,3456]{1,0:T(8,128)(2,1)}, u32[]{:S(2)}, u32[]{:S(2)}) %collective-permute-start.30) | collective-permute-done | bytes 884768 | tf_op jit(solution)/shard_map/ppermute | solution.py:92
  193.3 16.4 %attention_backward.1 = (f32[1024,256]{1,0:T(8,128)S(1)}, f32[1024,128]{1,0:T(8,128)S(1)}, bf16[1024,128]{1,0:T(8,128)(2,1)S(1)}) custom-call(s32[2]{0:T(128)S(1)} %copy-done.15, s32[4,1,256]{2,1,0:T(1,128)S(1)} %bitcast.11, bf16[1024,768]{1,0:T(8,128)(2,1)} %get-tuple-element.99.weights, bf16[1024,256]{1,0:T(8,128)(2,1)S(1)} %copy-done.22, ...), custom_call_target="tpu_custom_call" | custom-call | flops 16000000000 | bytes 8388608 | tf_op jit(solution)/shard_map/attention_backward/pallas_call | solution.py:884
  210.4 3.0 %collective-permute-done.33 = bf16[128,3456]{1,0:T(8,128)(2,1)S(1)} collective-permute-done((bf16[128,3456]{1,0:T(8,128)(2,1)S(1)}, bf16[128,3456]{1,0:T(8,128)(2,1)S(1)}, u32[]{:S(2)}, u32[]{:S(2)}) %collective-permute-start.33) | collective-permute-done | bytes 884768 | tf_op jit(solution)/shard_map/ppermute | solution.py:92
  213.4 2.8 %add_convert_fusion = (bf16[128,3456]{1,0:T(8,128)(2,1)}, bf16[128,3456]{1,0:T(8,128)(2,1)S(1)}) fusion(bf16[128,3456]{1,0:T(8,128)(2,1)S(1)} %collective-permute-done.33, bf16[512,3456]{1,0:T(8,128)(2,1)} %get-tuple-element.134, bf16[128,3456]{1,0:T(8,128)(2,1)S(1)} %collective-permute-done.32), kind=kLoop, calls=%fused_computation | loop fusion | flops 3538944 | bytes 5308416 | tf_op jit(solution)/shard_map/convert_element_type | solution.py:117
  218.2 10.8 %backward_end.1 = (bf16[1152,768]{1,0:T(8,128)(2,1)}, bf16[64,768]{1,0:T(8,128)(2,1)S(1)}, bf16[80,768]{1,0:T(8,128)(2,1)S(1)}, bf16[512,1024]{1,0:T(8,128)(2,1)...) custom-call(s32[2]{0:T(128)S(1)} %copy-done.15, bf16[1024,1024]{1,0:T(8,128)(2,1)} %arrange.1.tokens, ...), custom_call_target="tpu_custom_call" | custom-call | flops 8999999488 | bytes 14680064 | tf_op jit(solution)/shard_map/backward_end/pallas_call | solution.py:911
  231.2 7.2 %collective-permute-done.36 = bf16[64,768]{1,0:T(8,128)(2,1)S(1)} collective-permute-done((bf16[64,768]{1,0:T(8,128)(2,1)S(1)}, bf16[64,768]{1,0:T(8,128)(2,1)S(1)}, u32[]{:S(2)}, u32[]{:S(2)}) %collective-permute-start.36) | collective-permute-done | bytes 98336 | tf_op jit(solution)/shard_map/ppermute | solution.py:92
  241.9 4.1 %collective-permute-done.42 = bf16[144,768]{1,0:T(8,128)(2,1)S(1)} collective-permute-done((bf16[144,768]{1,0:T(8,128)(2,1)S(1)}, bf16[144,768]{1,0:T(8,128)(2,1)S(1)}, u32[]{:S(2)}, u32[]{:S(2)}) %collective-permute-start.42) | collective-permute-done | bytes 221216 | tf_op jit(solution)/shard_map/ppermute | solution.py:92
  248.5 4.6 %collective-permute-done.43 = bf16[144,768]{1,0:T(8,128)(2,1)S(1)} collective-permute-done((bf16[144,768]{1,0:T(8,128)(2,1)S(1)}, bf16[144,768]{1,0:T(8,128)(2,1)S(1)}, u32[]{:S(2)}, u32[]{:S(2)}) %collective-permute-start.43) | collective-permute-done | bytes 221216 | tf_op jit(solution)/shard_map/ppermute | solution.py:92
  259.1 2.2 collective-permute-done.41
  263.4 3.9 %collective-permute-done.44.up = bf16[144,768]{1,0:T(8,128)(2,1)S(1)} collective-permute-done((bf16[144,768]{1,0:T(8,128)(2,1)S(1)}, bf16[144,768]{1,0:T(8,128)(2,1)S(1)}, u32[]{:S(2)}, u32[]{:S(2)}) %collective-permute-start.44) | collective-permute-done | bytes 221216 | tf_op jit(solution)/shard_map/ppermute | solution.py:92
  271.3 2.0 input_back.1
  (197 shorter events, 75.3 us)
Async XLA Ops:
  3.6 8.7 %collective-permute-start.1 = (bf16[144,768]{1,0:T(8,128)(2,1)}, bf16[144,768]{1,0:T(8,128)(2,1)S(1)}, u32[]{:S(2)}, u32[]{:S(2)}) collective-permute-start(bf16[144,768]{1,0:T(8,128)(2,1)} %pack.1.p0), channel_id=1, source_target_pairs={{8,0},{16,8},{24,16},{28,24},{20,28},{12,20},{4,12},{0,4},{9,1},{1... | collective-permute-start | bytes 663560 | tf_op jit(solution)/shard_map/ppermute | solution.py:65
  36.0 23.1 %collective-permute-start.9 = (bf16[128,3456]{1,0:T(8,128)(2,1)S(1)}, bf16[128,3456]{1,0:T(8,128)(2,1)S(1)}, u32[]{:S(2)}, u32[]{:S(2)}) collective-permute-start(bf16[128,3456]{1,0:T(8,128)(2,1)S(1)} %pack_ffn.1.refs_0_), channel_id=1, source_target_pairs={{0,8},{8,16},{16,24},{24,28},{28,20},{20,12},{12,4},{4,0},{1,9},{9... | collective-permute-start | bytes 2654216 | tf_op jit(solution)/shard_map/ppermute | solution.py:65
  37.5 23.2 %collective-permute-start.10 = (bf16[128,3456]{1,0:T(8,128)(2,1)S(1)}, bf16[128,3456]{1,0:T(8,128)(2,1)S(1)}, u32[]{:S(2)}, u32[]{:S(2)}) collective-permute-start(bf16[128,3456]{1,0:T(8,128)(2,1)S(1)} %pack_ffn.1.refs_0_), channel_id=1, source_target_pairs={{8,0},{16,8},{24,16},{28,24},{20,28},{12,20},{4,12},{0,4},{9,1},{1... | collective-permute-start | bytes 2654216 | tf_op jit(solution)/shard_map/ppermute | solution.py:65
  59.1 22.1 %collective-permute-start.12 = (bf16[128,3456]{1,0:T(8,128)(2,1)S(1)}, bf16[128,3456]{1,0:T(8,128)(2,1)S(1)}, u32[]{:S(2)}, u32[]{:S(2)}) collective-permute-start(bf16[128,3456]{1,0:T(8,128)(2,1)S(1)} %collective-permute-done.9.refs_8_), channel_id=1, source_target_pairs={{0,8},{8,16},{16,24},{24,28},{28,20},{20,12},{12,4},{4,0},{1,9},{9... | collective-permute-start | bytes 2654216 | tf_op jit(solution)/shard_map/ppermute | solution.py:65
  60.8 22.0 %collective-permute-start.13 = (bf16[128,3456]{1,0:T(8,128)(2,1)S(1)}, bf16[128,3456]{1,0:T(8,128)(2,1)S(1)}, u32[]{:S(2)}, u32[]{:S(2)}) collective-permute-start(bf16[128,3456]{1,0:T(8,128)(2,1)S(1)} %collective-permute-done.10.refs_1_), channel_id=1, source_target_pairs={{8,0},{16,8},{24,16},{28,24},{20,28},{12,20},{4,12},{0,4},{9,1},{1... | collective-permute-start | bytes 2654216 | tf_op jit(solution)/shard_map/ppermute | solution.py:65
  62.0 21.2 %collective-permute-start.11 = (bf16[256,1024]{1,0:T(8,128)(2,1)S(1)}, bf16[256,1024]{1,0:T(8,128)(2,1)S(1)}, u32[]{:S(2)}, u32[]{:S(2)}) collective-permute-start(bf16[256,1024]{1,0:T(8,128)(2,1)S(1)} %add_convert_fusion.9), channel_id=1, source_target_pairs={{0,2},{1,3},{2,0},{3,1},{4,6},{5,7},{6,4},{7,5},{8,10},{9,11},{10,... | collective-permute-start | bytes 1572872 | tf_op jit(solution)/shard_map/ppermute | solution.py:122
  81.2 21.2 %collective-permute-start.18 = (bf16[128,3456]{1,0:T(8,128)(2,1)S(1)}, bf16[128,3456]{1,0:T(8,128)(2,1)S(1)}, u32[]{:S(2)}, u32[]{:S(2)}) collective-permute-start(bf16[128,3456]{1,0:T(8,128)(2,1)S(1)} %collective-permute-done.12.refs_7_), channel_id=1, source_target_pairs={{0,8},{8,16},{16,24},{24,28},{28,20},{20,12},{12,4},{4,0},{1,9},{9... | collective-permute-start | bytes 2654216 | tf_op jit(solution)/shard_map/ppermute | solution.py:65
  82.8 21.3 %collective-permute-start.17 = (bf16[128,3456]{1,0:T(8,128)(2,1)S(1)}, bf16[128,3456]{1,0:T(8,128)(2,1)S(1)}, u32[]{:S(2)}, u32[]{:S(2)}) collective-permute-start(bf16[128,3456]{1,0:T(8,128)(2,1)S(1)} %collective-permute-done.13.refs_2_), channel_id=1, source_target_pairs={{8,0},{16,8},{24,16},{28,24},{20,28},{12,20},{4,12},{0,4},{9,1},{1... | collective-permute-start | bytes 2654216 | tf_op jit(solution)/shard_map/ppermute | solution.py:65
  84.7 13.3 %collective-permute-start.15 = (bf16[256,1024]{1,0:T(8,128)(2,1)S(1)}, bf16[256,1024]{1,0:T(8,128)(2,1)}, u32[]{:S(2)}, u32[]{:S(2)}) collective-permute-start(bf16[256,1024]{1,0:T(8,128)(2,1)S(1)} %get-tuple-element.110.mine), channel_id=1, source_target_pairs={{0,2},{1,3},{2,0},{3,1},{4,6},{5,7},{6,4},{7,5},{8,10},{9,11},{10,... | collective-permute-start | bytes 1572872 | tf_op jit(solution)/shard_map/ppermute | solution.py:122
  86.3 24.5 %collective-permute-start.14 = (bf16[256,1024]{1,0:T(8,128)(2,1)S(1)}, bf16[256,1024]{1,0:T(8,128)(2,1)}, u32[]{:S(2)}, u32[]{:S(2)}) collective-permute-start(bf16[256,1024]{1,0:T(8,128)(2,1)S(1)} %get-tuple-element.110.mine), channel_id=1, source_target_pairs={{0,1},{1,0},{2,3},{3,2},{4,5},{5,4},{6,7},{7,6},{8,9},{9,8},{10,11... | collective-permute-start | bytes 1572872 | tf_op jit(solution)/shard_map/ppermute | solution.py:122
  98.0 12.9 %collective-permute-start.16 = (bf16[256,1024]{1,0:T(8,128)(2,1)}, bf16[256,1024]{1,0:T(8,128)(2,1)}, u32[]{:S(2)}, u32[]{:S(2)}) collective-permute-start(bf16[256,1024]{1,0:T(8,128)(2,1)} %collective-permute-done.15.far), channel_id=1, source_target_pairs={{0,1},{1,0},{2,3},{3,2},{4,5},{5,4},{6,7},{7,6},{8,9},{9,8},{10,11... | collective-permute-start | bytes 1572872 | tf_op jit(solution)/shard_map/ppermute | solution.py:122
  102.4 11.0 %collective-permute-start.19 = (bf16[64,3456]{1,0:T(8,128)(2,1)S(1)}, bf16[64,3456]{1,0:T(8,128)(2,1)}, u32[]{:S(2)}, u32[]{:S(2)}) collective-permute-start(bf16[64,3456]{1,0:T(8,128)(2,1)S(1)} %slice.137), channel_id=1, source_target_pairs={{0,8},{8,16},{16,24},{24,28},{28,20},{20,12},{12,4},{4,0},{1,9},{9... | collective-permute-start | bytes 1327112 | tf_op jit(solution)/shard_map/ppermute | solution.py:65
  105.0 10.7 %collective-permute-start.20 = (bf16[64,3456]{1,0:T(8,128)(2,1)S(1)}, bf16[64,3456]{1,0:T(8,128)(2,1)}, u32[]{:S(2)}, u32[]{:S(2)}) collective-permute-start(bf16[64,3456]{1,0:T(8,128)(2,1)S(1)} %slice.138), channel_id=1, source_target_pairs={{8,0},{16,8},{24,16},{28,24},{20,28},{12,20},{4,12},{0,4},{9,1},{1... | collective-permute-start | bytes 1327112 | tf_op jit(solution)/shard_map/ppermute | solution.py:65
  144.6 15.5 %collective-permute-start.21 = (bf16[512,1024]{1,0:T(8,128)(2,1)}, bf16[512,1024]{1,0:T(8,128)(2,1)S(1)}, u32[]{:S(2)}, u32[]{:S(2)}) collective-permute-start(bf16[512,1024]{1,0:T(8,128)(2,1)} %get-tuple-element.114), channel_id=1, source_target_pairs={{0,1},{1,0},{2,3},{3,2},{4,5},{5,4},{6,7},{7,6},{8,9},{9,8},{10,11... | collective-permute-start | bytes 3145736 | tf_op jit(solution)/shard_map/ppermute | solution.py:122
  148.7 14.0 %collective-permute-start.23 = (bf16[256,1024]{1,0:T(8,128)(2,1)S(1)}, bf16[256,1024]{1,0:T(8,128)(2,1)S(1)}, u32[]{:S(2)}, u32[]{:S(2)}) collective-permute-start(bf16[256,1024]{1,0:T(8,128)(2,1)S(1)} %add_convert_fusion.8), channel_id=1, source_target_pairs={{0,2},{1,3},{2,0},{3,1},{4,6},{5,7},{6,4},{7,5},{8,10},{9,11},{10,... | collective-permute-start | bytes 1572872 | tf_op jit(solution)/shard_map/ppermute | solution.py:122
  150.2 15.8 %collective-permute-start.28 = (bf16[64,3456]{1,0:T(8,128)(2,1)}, bf16[64,3456]{1,0:T(8,128)(2,1)S(1)}, u32[]{:S(2)}, u32[]{:S(2)}) collective-permute-start(bf16[64,3456]{1,0:T(8,128)(2,1)} %get-tuple-element.130), channel_id=1, source_target_pairs={{0,8},{8,16},{16,24},{24,28},{28,20},{20,12},{12,4},{4,0},{1,9},{9... | collective-permute-start | bytes 1327112 | tf_op jit(solution)/shard_map/ppermute | solution.py:92
  151.8 14.3 %collective-permute-start.29 = (bf16[64,3456]{1,0:T(8,128)(2,1)}, bf16[64,3456]{1,0:T(8,128)(2,1)S(1)}, u32[]{:S(2)}, u32[]{:S(2)}) collective-permute-start(bf16[64,3456]{1,0:T(8,128)(2,1)} %get-tuple-element.131), channel_id=1, source_target_pairs={{8,0},{16,8},{24,16},{28,24},{20,28},{12,20},{4,12},{0,4},{9,1},{1... | collective-permute-start | bytes 1327112 | tf_op jit(solution)/shard_map/ppermute | solution.py:92
  164.4 28.9 %collective-permute-start.26 = (bf16[256,1024]{1,0:T(8,128)(2,1)S(1)}, bf16[256,1024]{1,0:T(8,128)(2,1)S(1)}, u32[]{:S(2)}, u32[]{:S(2)}) collective-permute-start(bf16[256,1024]{1,0:T(8,128)(2,1)S(1)} %get-tuple-element.139.mine), channel_id=1, source_target_pairs={{0,1},{1,0},{2,3},{3,2},{4,5},{5,4},{6,7},{7,6},{8,9},{9,8},{10,11... | collective-permute-start | bytes 1572872 | tf_op jit(solution)/shard_map/ppermute | solution.py:122
  164.5 14.3 %collective-permute-start.24 = (bf16[256,1024]{1,0:T(8,128)(2,1)S(1)}, bf16[256,1024]{1,0:T(8,128)(2,1)S(1)}, u32[]{:S(2)}, u32[]{:S(2)}) collective-permute-start(bf16[256,1024]{1,0:T(8,128)(2,1)S(1)} %get-tuple-element.139.mine), channel_id=1, source_target_pairs={{0,2},{1,3},{2,0},{3,1},{4,6},{5,7},{6,4},{7,5},{8,10},{9,11},{10,... | collective-permute-start | bytes 1572872 | tf_op jit(solution)/shard_map/ppermute | solution.py:122
  166.2 21.9 %collective-permute-start.30 = (bf16[128,3456]{1,0:T(8,128)(2,1)S(1)}, bf16[128,3456]{1,0:T(8,128)(2,1)}, u32[]{:S(2)}, u32[]{:S(2)}) collective-permute-start(bf16[128,3456]{1,0:T(8,128)(2,1)S(1)} %add_convert_fusion.5), channel_id=1, source_target_pairs={{0,8},{8,16},{16,24},{24,28},{28,20},{20,12},{12,4},{4,0},{1,9},{9... | collective-permute-start | bytes 2654216 | tf_op jit(solution)/shard_map/ppermute | solution.py:92
  169.1 22.0 %collective-permute-start.31 = (bf16[128,3456]{1,0:T(8,128)(2,1)S(1)}, bf16[128,3456]{1,0:T(8,128)(2,1)}, u32[]{:S(2)}, u32[]{:S(2)}) collective-permute-start(bf16[128,3456]{1,0:T(8,128)(2,1)S(1)} %add_convert_fusion.3), channel_id=1, source_target_pairs={{8,0},{16,8},{24,16},{28,24},{20,28},{12,20},{4,12},{0,4},{9,1},{1... | collective-permute-start | bytes 2654216 | tf_op jit(solution)/shard_map/ppermute | solution.py:92
  178.8 14.4 %collective-permute-start.25 = (bf16[256,1024]{1,0:T(8,128)(2,1)}, bf16[256,1024]{1,0:T(8,128)(2,1)S(1)}, u32[]{:S(2)}, u32[]{:S(2)}) collective-permute-start(bf16[256,1024]{1,0:T(8,128)(2,1)} %add_convert_fusion.7), channel_id=1, source_target_pairs={{0,2},{1,3},{2,0},{3,1},{4,6},{5,7},{6,4},{7,5},{8,10},{9,11},{10,... | collective-permute-start | bytes 1572872 | tf_op jit(solution)/shard_map/ppermute | solution.py:122
  180.3 12.9 %collective-permute-start.27 = (bf16[256,1024]{1,0:T(8,128)(2,1)S(1)}, bf16[256,1024]{1,0:T(8,128)(2,1)S(1)}, u32[]{:S(2)}, u32[]{:S(2)}) collective-permute-start(bf16[256,1024]{1,0:T(8,128)(2,1)S(1)} %collective-permute-done.24.far), channel_id=1, source_target_pairs={{0,1},{1,0},{2,3},{3,2},{4,5},{5,4},{6,7},{7,6},{8,9},{9,8},{10,11... | collective-permute-start | bytes 1572872 | tf_op jit(solution)/shard_map/ppermute | solution.py:122
  189.5 20.9 %collective-permute-start.32 = (bf16[128,3456]{1,0:T(8,128)(2,1)S(1)}, bf16[128,3456]{1,0:T(8,128)(2,1)S(1)}, u32[]{:S(2)}, u32[]{:S(2)}) collective-permute-start(bf16[128,3456]{1,0:T(8,128)(2,1)S(1)} %add_convert_fusion.4), channel_id=1, source_target_pairs={{0,8},{8,16},{16,24},{24,28},{28,20},{20,12},{12,4},{4,0},{1,9},{9... | collective-permute-start | bytes 2654216 | tf_op jit(solution)/shard_map/ppermute | solution.py:92
  192.8 20.7 %collective-permute-start.33 = (bf16[128,3456]{1,0:T(8,128)(2,1)S(1)}, bf16[128,3456]{1,0:T(8,128)(2,1)S(1)}, u32[]{:S(2)}, u32[]{:S(2)}) collective-permute-start(bf16[128,3456]{1,0:T(8,128)(2,1)S(1)} %add_convert_fusion.2), channel_id=1, source_target_pairs={{8,0},{16,8},{24,16},{28,24},{20,28},{12,20},{4,12},{0,4},{9,1},{1... | collective-permute-start | bytes 2654216 | tf_op jit(solution)/shard_map/ppermute | solution.py:92
  216.2 23.6 %collective-permute-start.39 = (bf16[128,3456]{1,0:T(8,128)(2,1)}, bf16[128,3456]{1,0:T(8,128)(2,1)S(1)}, u32[]{:S(2)}, u32[]{:S(2)}) collective-permute-start(bf16[128,3456]{1,0:T(8,128)(2,1)} %get-tuple-element.167), channel_id=1, source_target_pairs={{8,0},{16,8},{24,16},{28,24},{20,28},{12,20},{4,12},{0,4},{9,1},{1... | collective-permute-start | bytes 2654216 | tf_op jit(solution)/shard_map/ppermute | solution.py:92
  216.8 23.1 %collective-permute-start.38 = (bf16[128,3456]{1,0:T(8,128)(2,1)S(1)}, bf16[128,3456]{1,0:T(8,128)(2,1)S(1)}, u32[]{:S(2)}, u32[]{:S(2)}) collective-permute-start(bf16[128,3456]{1,0:T(8,128)(2,1)S(1)} %get-tuple-element.168), channel_id=1, source_target_pairs={{0,8},{8,16},{16,24},{24,28},{28,20},{20,12},{12,4},{4,0},{1,9},{9... | collective-permute-start | bytes 2654216 | tf_op jit(solution)/shard_map/ppermute | solution.py:92
  229.1 18.6 %collective-permute-start.34 = (bf16[512,1024]{1,0:T(8,128)(2,1)S(1)}, bf16[512,1024]{1,0:T(8,128)(2,1)S(1)}, u32[]{:S(2)}, u32[]{:S(2)}) collective-permute-start(bf16[512,1024]{1,0:T(8,128)(2,1)S(1)} %get-tuple-element.150), channel_id=1, source_target_pairs={{0,1},{1,0},{2,3},{3,2},{4,5},{5,4},{6,7},{7,6},{8,9},{9,8},{10,11... | collective-permute-start | bytes 3145736 | tf_op jit(solution)/shard_map/ppermute | solution.py:122
  229.2 9.6 %collective-permute-start.37 = (bf16[80,768]{1,0:T(8,128)(2,1)S(1)}, bf16[80,768]{1,0:T(8,128)(2,1)S(1)}, u32[]{:S(2)}, u32[]{:S(2)}) collective-permute-start(bf16[80,768]{1,0:T(8,128)(2,1)S(1)} %get-tuple-element.154), channel_id=1, source_target_pairs={{8,0},{16,8},{24,16},{28,24},{20,28},{12,20},{4,12},{0,4},{9,1},{1... | collective-permute-start | bytes 368648 | tf_op jit(solution)/shard_map/ppermute | solution.py:92
  229.8 8.6 %collective-permute-start.36 = (bf16[64,768]{1,0:T(8,128)(2,1)S(1)}, bf16[64,768]{1,0:T(8,128)(2,1)S(1)}, u32[]{:S(2)}, u32[]{:S(2)}) collective-permute-start(bf16[64,768]{1,0:T(8,128)(2,1)S(1)} %get-tuple-element.153), channel_id=1, source_target_pairs={{0,8},{8,16},{16,24},{24,28},{28,20},{20,12},{12,4},{4,0},{1,9},{9... | collective-permute-start | bytes 294920 | tf_op jit(solution)/shard_map/ppermute | solution.py:92
  247.9 13.4 %collective-permute-start.35 = (bf16[256,1024]{1,0:T(8,128)(2,1)S(1)}, bf16[256,1024]{1,0:T(8,128)(2,1)S(1)}, u32[]{:S(2)}, u32[]{:S(2)}) collective-permute-start(bf16[256,1024]{1,0:T(8,128)(2,1)S(1)} %add_convert_fusion.6), channel_id=1, source_target_pairs={{0,2},{1,3},{2,0},{3,1},{4,6},{5,7},{6,4},{7,5},{8,10},{9,11},{10,... | collective-permute-start | bytes 1572872 | tf_op jit(solution)/shard_map/ppermute | solution.py:122
  253.2 8.1 %collective-permute-start.41 = (bf16[144,768]{1,0:T(8,128)(2,1)S(1)}, bf16[144,768]{1,0:T(8,128)(2,1)S(1)}, u32[]{:S(2)}, u32[]{:S(2)}) collective-permute-start(bf16[144,768]{1,0:T(8,128)(2,1)S(1)} %get-tuple-element.170), channel_id=1, source_target_pairs={{0,8},{8,16},{16,24},{24,28},{28,20},{20,12},{12,4},{4,0},{1,9},{9... | collective-permute-start | bytes 663560 | tf_op jit(solution)/shard_map/ppermute | solution.py:92
  (57 other events, 621.4 us)
